TPU v7x, 512 devices: a whole 4x8x8 slice. The times are simulated.
512 devices in a mesh: seq: 64 (over y, x, core), mp: 8 (over z).
Axes of the slice: x: 4, y: 8, z: 8, core: 2. Of those that a mesh axis runs over, the one named last changes fastest.
Arguments:
- queries: bfloat16 [24576, 2048], P('seq', 'mp')
- neighbor_keys: bfloat16 [98304, 2048], P('seq', 'mp')
- neighbor_values: bfloat16 [98304, 2048], P('seq', 'mp'), may hold values from -6 to 6
- out_grad: bfloat16 [24576, 2048], P('seq', 'mp'), may hold values from -6 to 6
- neighbor_source: int32 [384, 4], P('seq'), may hold values from 0 to 63, as said below
- send_unit: int32 [64, 64, 1], P('seq'), may hold values from -1 to 23, as said below
Outputs:
- attended: bfloat16 [24576, 2048], P('seq', 'mp')
- query_grad: bfloat16 [24576, 2048], P('seq', 'mp')
- key_grad: bfloat16 [98304, 2048], P('seq', 'mp')
- value_grad: bfloat16 [98304, 2048], P('seq', 'mp')
Inputs may be any that keep to these rules, and one draw needn't show every extreme that they name: The 24 entries of the groups of one index of seq are distinct, so one owner sends one index at most 1 block; in every draw some owner sends some index 1 block. neighbor_source and send_unit describe the same assignment. `send_unit`: every one of an owner's 24 blocks fills exactly one slot; the other slots hold -1.
All inputs are finite; a program needn't handle non-finite values.
Results may differ from a plain program's by a relative error of at most 0.0072.
Values may be sent and summed in bfloat16 or wider, within the bound.
No kernel may reach another device: no remote copies, remote signals or barrier semaphores. Data moves between devices by JAX's collectives and lax.ppermute only.
A program may use at most 64 MiB of HBM per device.

v0:
```python
import jax
import jax.numpy as jnp
from jax import lax
from jax.sharding import PartitionSpec as P

HEAD_DIM = 128
GROUP = 64


def from_behind(value, axis, steps):
    count = lax.axis_size(axis)
    first, last = (max(0, -steps), min(count, count - steps))
    return lax.ppermute(value, axis, [(source, source + steps) for source in range(first, last)])


def heads_view(block_array):
    return block_array.reshape(
        block_array.shape[:-1] + (block_array.shape[-1] // HEAD_DIM, HEAD_DIM)
    )


def block_probs(query_blocks, key_blocks):
    score_scale = HEAD_DIM ** (-0.5)
    scores = (
        jnp.einsum(
            "bqhd,bkhd->bhqk",
            heads_view(query_blocks),
            heads_view(key_blocks),
            preferred_element_type=jnp.float32,
        )
        * score_scale
    )
    row_max = jnp.max(scores, axis=-1, keepdims=True)
    powers = jnp.exp(scores - row_max)
    return powers / jnp.sum(powers, axis=-1, keepdims=True)


def forward_blocks(query_blocks, key_blocks, value_blocks):
    probs_low = block_probs(query_blocks, key_blocks).astype(jnp.bfloat16)
    mixed = jnp.einsum(
        "bhqk,bkhd->bqhd", probs_low, heads_view(value_blocks), preferred_element_type=jnp.float32
    )
    return mixed.reshape(query_blocks.shape).astype(jnp.bfloat16)


def backward_blocks(query_blocks, key_blocks, value_blocks, grad_blocks):
    score_scale = HEAD_DIM ** (-0.5)
    attn_probs = block_probs(query_blocks, key_blocks)
    probs_low = attn_probs.astype(jnp.bfloat16)
    query_heads = heads_view(query_blocks)
    key_heads = heads_view(key_blocks)
    grad_heads = heads_view(grad_blocks)
    grad_probs = jnp.einsum(
        "bqhd,bkhd->bhqk", grad_heads, heads_view(value_blocks), preferred_element_type=jnp.float32
    )
    row_dot = jnp.sum(attn_probs * grad_probs, axis=-1, keepdims=True)
    grad_scores = (attn_probs * (grad_probs - row_dot) * score_scale).astype(jnp.bfloat16)
    query_part = jnp.einsum(
        "bhqk,bkhd->bqhd", grad_scores, key_heads, preferred_element_type=jnp.float32
    )
    key_part = jnp.einsum(
        "bhqk,bqhd->bkhd", grad_scores, query_heads, preferred_element_type=jnp.float32
    )
    value_part = jnp.einsum(
        "bhqk,bqhd->bkhd", probs_low, grad_heads, preferred_element_type=jnp.float32
    )
    return (
        query_part.reshape(query_blocks.shape).astype(jnp.bfloat16),
        key_part.reshape(key_blocks.shape),
        value_part.reshape(key_blocks.shape),
    )


def arrange_slots(received, source_flat, group_count, per_group):
    picked = jnp.take(received, source_flat, axis=0)
    return picked.reshape(group_count, per_group * received.shape[1], received.shape[2])


def local(queries, neighbor_keys, neighbor_values, out_grad, neighbor_source, send_unit):
    my_index = lax.axis_index("seq")
    tok_rows, col_count = queries.shape
    seq_total = tok_rows * lax.axis_size("seq")
    group_count = tok_rows // GROUP
    unit_count = neighbor_keys.shape[0] // GROUP
    per_group = neighbor_source.shape[1]
    slot_count = send_unit.shape[1] * send_unit.shape[2]
    send_table = send_unit[0].reshape(slot_count)
    source_flat = neighbor_source.reshape(unit_count)
    zero_value = jnp.zeros((), jnp.bfloat16)
    key_units = neighbor_keys.reshape(unit_count, GROUP, col_count)
    value_units = neighbor_values.reshape(unit_count, GROUP, col_count)
    send_used = (send_table >= 0)[:, None, None]
    send_pos = jnp.maximum(send_table, 0)
    key_send = jnp.where(send_used, jnp.take(key_units, send_pos, axis=0), zero_value)
    value_send = jnp.where(send_used, jnp.take(value_units, send_pos, axis=0), zero_value)
    key_recv, value_recv = (
        lax.all_to_all(key_send, "seq", split_axis=0, concat_axis=0, tiled=True),
        lax.all_to_all(value_send, "seq", split_axis=0, concat_axis=0, tiled=True),
    )
    key_slots = arrange_slots(key_recv, source_flat, group_count, per_group)
    value_slots = arrange_slots(value_recv, source_flat, group_count, per_group)
    ext_rows = tok_rows + GROUP
    offsets = jnp.arange(ext_rows, dtype=jnp.int32) - 1
    global_pos = my_index * tok_rows + offsets
    seq_live = jnp.remainder(global_pos, seq_total) >= GROUP - 1
    own_live = seq_live & (offsets >= 0) & (offsets < tok_rows)
    zero_row = jnp.zeros((1, col_count), jnp.bfloat16)
    zero_tail = jnp.zeros((GROUP - 1, col_count), jnp.bfloat16)
    grad_own = jnp.where(own_live[1 : tok_rows + 1, None], out_grad, zero_value)
    query_ext = jnp.concatenate([zero_row, queries, zero_tail], axis=0)
    grad_ext = jnp.concatenate([zero_row, grad_own, zero_tail], axis=0)
    query_blocks = query_ext.reshape(group_count + 1, GROUP, col_count)
    grad_blocks = grad_ext.reshape(group_count + 1, GROUP, col_count)
    prior_keys, prior_values = from_behind((key_slots[-1], value_slots[-1]), "seq", 1)
    key_blocks = jnp.concatenate([prior_keys[None], key_slots], axis=0)
    value_blocks = jnp.concatenate([prior_values[None], value_slots], axis=0)
    mixed = forward_blocks(query_blocks, key_blocks, value_blocks).reshape(ext_rows, col_count)
    attended = jnp.where(own_live[:, None], mixed, zero_value)[1 : tok_rows + 1]
    key_blocks = jnp.concatenate([prior_keys[None], key_slots], axis=0)
    value_blocks = jnp.concatenate([prior_values[None], value_slots], axis=0)
    query_part, key_part, value_part = backward_blocks(
        query_blocks, key_blocks, value_blocks, grad_blocks
    )
    query_grad = query_part.reshape(ext_rows, col_count)[1 : tok_rows + 1]
    later_keys, later_values = (
        from_behind(key_part[0].astype(jnp.bfloat16), "seq", -1).astype(jnp.float32),
        from_behind(value_part[0].astype(jnp.bfloat16), "seq", -1).astype(jnp.float32),
    )
    key_slot_grad = key_part[1:].at[-1].add(later_keys)
    value_slot_grad = value_part[1:].at[-1].add(later_values)
    key_grad_units = key_slot_grad.astype(jnp.bfloat16).reshape(unit_count, GROUP, col_count)
    value_grad_units = value_slot_grad.astype(jnp.bfloat16).reshape(unit_count, GROUP, col_count)
    slot_match = source_flat[None, :] == jnp.arange(slot_count, dtype=jnp.int32)[:, None]
    slot_which = jnp.sum(
        jnp.where(slot_match, jnp.arange(unit_count, dtype=jnp.int32)[None, :], 0), axis=1
    )
    slot_used = jnp.any(slot_match, axis=1)[:, None, None]
    key_return = jnp.where(slot_used, jnp.take(key_grad_units, slot_which, axis=0), zero_value)
    value_return = jnp.where(slot_used, jnp.take(value_grad_units, slot_which, axis=0), zero_value)
    key_back, value_back = (
        lax.all_to_all(key_return, "seq", split_axis=0, concat_axis=0, tiled=True),
        lax.all_to_all(value_return, "seq", split_axis=0, concat_axis=0, tiled=True),
    )
    unit_match = send_table[None, :] == jnp.arange(unit_count, dtype=jnp.int32)[:, None]
    unit_which = jnp.sum(
        jnp.where(unit_match, jnp.arange(slot_count, dtype=jnp.int32)[None, :], 0), axis=1
    )
    unit_used = jnp.any(unit_match, axis=1)[:, None, None]
    key_grad = jnp.where(unit_used, jnp.take(key_back, unit_which, axis=0), zero_value).reshape(
        unit_count * GROUP, col_count
    )
    value_grad = jnp.where(unit_used, jnp.take(value_back, unit_which, axis=0), zero_value).reshape(
        unit_count * GROUP, col_count
    )
    return (attended, query_grad, key_grad, value_grad)


def solution(mesh):
    return jax.shard_map(
        local,
        mesh=mesh,
        in_specs=(
            P("seq", "mp"),
            P("seq", "mp"),
            P("seq", "mp"),
            P("seq", "mp"),
            P("seq", None),
            P("seq", None, None),
        ),
        out_specs=(P("seq", "mp"), P("seq", "mp"), P("seq", "mp"), P("seq", "mp")),
        check_vma=False,
    )
```

profile of v0, /device:TPU:1, one launch (start us, length us, event | category | flops | bytes accessed | tf_op | source)
XLA Modules:
  0.0 300.0 jit_solution(7118292113123352143)
XLA Ops:
  3.7 3.2 %gather_fusion = bf16[64,64,256]{2,1,0:T(8,128)(2,1)} fusion(bf16[24,64,256]{2,1,0:T(8,128)(2,1)} %bitcast.47, s32[1024]{0:T(1024)S(1)} %pad_clamp_fusion.3), kind=kCustom, calls=%fused_computation.clone | custom fusion | bytes 4194560 | tf_op jit(solution)/shard_map/jit(_take)/gather | solution.py:95
  6.8 3.1 %select_select_fusion.2 = (bf16[64,64,256]{2,1,0:T(8,128)(2,1)S(1)}, bf16[64,64,256]{2,1,0:T(8,128)(2,1)}) fusion(bf16[64,64,256]{2,1,0:T(8,128)(2,1)S(1)} %gather_fusion.2, pred[64]{0:T(512)(128)(4,1)S(1)} %get-tuple-element.41, pred[64]{0:T(512)(128)(4,1)S(1)} %get-tuple-element.40, bf16[64,64,256]{2,1,0:T(8,128)(2,1)} %gather_fusion), kind=kLoop, calls=%fused_computation.12 | loop fusion | flops 4194304 | bytes 8388736 | tf_op jit(solution)/shard_map/jit(_where)/select_n | solution.py:94
  10.0 61.2 %all_to_all.20 = bf16[64,64,256]{2,1,0:T(8,128)(2,1)} all-to-all(bf16[64,64,256]{2,1,0:T(8,128)(2,1)S(1)} %get-tuple-element.36), channel_id=1, replica_groups=mesh['seq'=64,'mp'=8] {'seq'}, dimensions={0} | all-to-all | bytes 4194304 | tf_op jit(solution)/shard_map/all_to_all | solution.py:97
  71.1 7.2 %all-to-all-start = ((bf16[64,64,256]{2,1,0:T(8,128)(2,1)}), bf16[64,64,256]{2,1,0:T(8,128)(2,1)S(1)}, u32[]{:S(2)}, u32[]{:S(2)}) async-start(bf16[64,64,256]{2,1,0:T(8,128)(2,1)} %get-tuple-element.37), calls=%async_computation | async-start | bytes 4194304 | tf_op jit(solution)/shard_map/all_to_all | solution.py:98
  79.4 3.1 %gather_fusion.3 = bf16[24,64,256]{2,1,0:T(8,128)(2,1)} fusion(bf16[64,64,256]{2,1,0:T(8,128)(2,1)} %all_to_all.20, s32[1024]{0:T(1024)S(1)} %pad_clamp_fusion.2), kind=kCustom, calls=%fused_computation.5.clone | custom fusion | bytes 1572960 | tf_op jit(solution)/shard_map/jit(_take)/gather | solution.py:75
  82.5 45.5 %all-to-all-done = bf16[64,64,256]{2,1,0:T(8,128)(2,1)S(1)} async-done(((bf16[64,64,256]{2,1,0:T(8,128)(2,1)}), bf16[64,64,256]{2,1,0:T(8,128)(2,1)S(1)}, u32[]{:S(2)}, u32[]{:S(2)}) %all-to-all-start) | async-done | bytes 2097184 | tf_op jit(solution)/shard_map/all_to_all | solution.py:98
  131.7 5.1 %collective-permute-start = (bf16[256,256]{1,0:T(8,128)(2,1)}, bf16[256,256]{1,0:T(8,128)(2,1)S(1)}, u32[]{:S(2)}, u32[]{:S(2)}) collective-permute-start(bf16[256,256]{1,0:T(8,128)(2,1)} %bitcast.2), channel_id=1, source_target_pairs={{0,8},{8,16},{16,24},{24,32},{32,40},{40,48},{48,56},{56,64},{64,7... | collective-permute-start | bytes 393224 | tf_op jit(solution)/shard_map/ppermute | solution.py:13
  137.5 1.9 collective-permute-start.1
  142.8 2.5 fusion.49
  145.3 1.7 convolution_bitcast_fusion
  149.1 2.8 collective-permute-start.3
  152.3 8.0 %convolution_bitcast_fusion.1 = f32[7,256,2,128]{1,3,2,0:T(8,128)} fusion(f32[7,2,64,256]{3,2,1,0:T(8,128)S(1)} %fusion.14, bf16[7,64,2,128]{3,2,1,0:T(2,128)(2,1)S(1)} %copy-done.6, f32[7,2,64,256]{3,2,1,0:T(8,128)} %get-tuple-element.43, f32[7,2,64]{2,1,0:T(2,128)S(1)} %get-tuple-element.42), kind=kOutput, calls=%fused_computation.15 | convolution fusion | flops 60327040 | bytes 3902976 | tf_op jit(solution)/shard_map/bhqk,bqhd->bkhd/dot_general | solution.py:61
  162.0 1.7 slice.125
  168.9 1.9 collective-permute-start.2
  171.8 2.0 gather_fusion.6
  175.2 2.0 gather_fusion.4
  177.2 3.6 %select_select_fusion = (bf16[64,64,256]{2,1,0:T(8,128)(2,1)S(1)}, bf16[64,64,256]{2,1,0:T(8,128)(2,1)}) fusion(bf16[64,64,256]{2,1,0:T(8,128)(2,1)} %gather_fusion.6, pred[64]{0:T(512)(128)(4,1)S(1)} %get-tuple-element.44, pred[64]{0:T(512)(128)(4,1)S(1)} %fusion.25, bf16[64,64,256]{2,1,0:T(8,128)(2,1)} %gather_fusion.4), kind=kLoop, calls=%fused_computation.10 | loop fusion | flops 4194304 | bytes 8388736 | tf_op jit(solution)/shard_map/jit(_where)/select_n | solution.py:139
  180.8 58.0 %all_to_all.21 = bf16[64,64,256]{2,1,0:T(8,128)(2,1)} all-to-all(bf16[64,64,256]{2,1,0:T(8,128)(2,1)S(1)} %get-tuple-element.34), channel_id=1, replica_groups=mesh['seq'=64,'mp'=8] {'seq'}, dimensions={0} | all-to-all | bytes 4194304 | tf_op jit(solution)/shard_map/all_to_all | solution.py:142
  238.8 7.2 %all-to-all-start.2 = ((bf16[64,64,256]{2,1,0:T(8,128)(2,1)}), bf16[64,64,256]{2,1,0:T(8,128)(2,1)S(1)}, u32[]{:S(2)}, u32[]{:S(2)}) async-start(bf16[64,64,256]{2,1,0:T(8,128)(2,1)} %get-tuple-element.35), calls=%async_computation.2 | async-start | bytes 4194304 | tf_op jit(solution)/shard_map/all_to_all | solution.py:141
  246.3 1.7 fusion.8
  248.3 7.0 %fusion.9 = bf16[7,64,2,128]{3,1,2,0:T(8,128)(2,1)S(1)} fusion(f32[7,2,64,256]{3,2,1,0:T(8,128)} %copy-done.2, bf16[6,256,2,128]{3,1,2,0:T(8,128)(2,1)} %copy-done.3, bf16[1,256,2,128]{3,1,2,0:T(8,128)(2,1)} %copy-done.9, f32[7,2,64,256]{3,2,1,0:T(8,128)} %get-tuple-element.43, f32[7,2,64]{2,1,0:T(2,128)S(1)} %copy-done.15), kind=kOutput, calls=%fused_computation.26 | convolution fusion | flops 62276736 | bytes 2985472 | tf_op jit(solution)/shard_map/bhqk,bkhd->bqhd/dot_general | solution.py:58
  257.1 3.1 %gather_fusion.7 = bf16[24,64,256]{2,1,0:T(8,128)(2,1)} fusion(bf16[64,64,256]{2,1,0:T(8,128)(2,1)} %all_to_all.21, s32[1024]{0:T(1024)S(1)} %pad_clamp_fusion), kind=kCustom, calls=%fused_computation.7.clone | custom fusion | bytes 1572960 | tf_op jit(solution)/shard_map/jit(_take)/gather | solution.py:152
  260.2 35.5 %all-to-all-done.2 = bf16[64,64,256]{2,1,0:T(8,128)(2,1)S(1)} async-done(((bf16[64,64,256]{2,1,0:T(8,128)(2,1)}), bf16[64,64,256]{2,1,0:T(8,128)(2,1)S(1)}, u32[]{:S(2)}, u32[]{:S(2)}) %all-to-all-start.2) | async-done | bytes 2097184 | tf_op jit(solution)/shard_map/all_to_all | solution.py:141
  297.2 2.8 select_select_fusion.4
  (96 shorter events, 27.3 us)
Async XLA Ops:
  0.6 2.4 copy-start
  2.2 76.3 %copy-start.11 = (s32[24]{0:T(128)}, s32[24]{0:T(128)S(1)}, u32[]{:S(2)}) copy-start(s32[24]{0:T(128)S(1)} %reshape.173) | copy-start | bytes 292
  71.1 7.9 %copy-start.7 = (bf16[384,256]{1,0:T(8,128)(2,1)S(1)}, bf16[384,256]{1,0:T(8,128)(2,1)}, u32[]{:S(2)}) copy-start(bf16[384,256]{1,0:T(8,128)(2,1)} %param.17) | copy-start | bytes 589828
  71.1 8.0 %copy-start.8 = (bf16[384,256]{1,0:T(8,128)(2,1)S(1)}, bf16[384,256]{1,0:T(8,128)(2,1)}, u32[]{:S(2)}) copy-start(bf16[384,256]{1,0:T(8,128)(2,1)} %param.14) | copy-start | bytes 589828
  71.1 56.8 %all-to-all-start = ((bf16[64,64,256]{2,1,0:T(8,128)(2,1)}), bf16[64,64,256]{2,1,0:T(8,128)(2,1)S(1)}, u32[]{:S(2)}, u32[]{:S(2)}) async-start(bf16[64,64,256]{2,1,0:T(8,128)(2,1)} %get-tuple-element.37), calls=%async_computation | async-start | bytes 4194304 | tf_op jit(solution)/shard_map/all_to_all | solution.py:98
  79.4 50.1 %copy-start.13 = (pred[24]{0:T(512)(128)(4,1)S(1)}, pred[24]{0:T(512)(128)(4,1)}, u32[]{:S(2)}) copy-start(pred[24]{0:T(512)(128)(4,1)} %compare_and_fusion.2) | copy-start | bytes 76
  129.5 10.8 %copy-start.12 = (s32[24]{0:T(128)S(1)}, s32[24]{0:T(128)}, u32[]{:S(2)}) copy-start(s32[24]{0:T(128)} %copy-done.11) | copy-start | bytes 292
  131.7 9.3 %collective-permute-start = (bf16[256,256]{1,0:T(8,128)(2,1)}, bf16[256,256]{1,0:T(8,128)(2,1)S(1)}, u32[]{:S(2)}, u32[]{:S(2)}) collective-permute-start(bf16[256,256]{1,0:T(8,128)(2,1)} %bitcast.2), channel_id=1, source_target_pairs={{0,8},{8,16},{16,24},{24,32},{32,40},{40,48},{48,56},{56,64},{64,7... | collective-permute-start | bytes 393224 | tf_op jit(solution)/shard_map/ppermute | solution.py:13
  137.5 4.2 %collective-permute-start.1 = (bf16[256,256]{1,0:T(8,128)(2,1)}, bf16[256,256]{1,0:T(8,128)(2,1)}, u32[]{:S(2)}, u32[]{:S(2)}) collective-permute-start(bf16[256,256]{1,0:T(8,128)(2,1)} %bitcast.5), channel_id=1, source_target_pairs={{0,8},{8,16},{16,24},{24,32},{32,40},{40,48},{48,56},{56,64},{64,7... | collective-permute-start | bytes 393224 | tf_op jit(solution)/shard_map/ppermute | solution.py:13
  140.9 11.0 %copy-start.1 = (bf16[6,256,2,128]{3,1,2,0:T(8,128)(2,1)}, bf16[6,256,2,128]{3,1,2,0:T(8,128)(2,1)S(1)}, u32[]{:S(2)}) copy-start(bf16[6,256,2,128]{3,1,2,0:T(8,128)(2,1)S(1)} %copy.52) | copy-start | bytes 2359300
  141.0 6.0 %copy-start.3 = (bf16[6,256,2,128]{3,1,2,0:T(8,128)(2,1)}, bf16[6,256,2,128]{3,1,2,0:T(8,128)(2,1)S(1)}, u32[]{:S(2)}) copy-start(bf16[6,256,2,128]{3,1,2,0:T(8,128)(2,1)S(1)} %copy.55) | copy-start | bytes 2359300
  142.8 4.2 %copy-start.9 = (bf16[1,256,2,128]{3,1,2,0:T(8,128)(2,1)}, bf16[1,256,2,128]{3,1,2,0:T(8,128)(2,1)S(1)}, u32[]{:S(2)}) copy-start(bf16[1,256,2,128]{3,1,2,0:T(8,128)(2,1)S(1)} %copy.54) | copy-start | bytes 393220
  145.3 7.0 %copy-start.14 = (f32[7,2,64]{2,1,0:T(2,128)}, f32[7,2,64]{2,1,0:T(2,128)S(1)}, u32[]{:S(2)}) copy-start(f32[7,2,64]{2,1,0:T(2,128)S(1)} %get-tuple-element.42) | copy-start | bytes 10756
  147.1 1.2 copy-start.4
  148.3 4.0 %copy-start.6 = (bf16[7,64,2,128]{3,2,1,0:T(2,128)(2,1)S(1)}, bf16[7,64,2,128]{3,2,1,0:T(2,128)(2,1)}, u32[]{:S(2)}) copy-start(bf16[7,64,2,128]{3,2,1,0:T(2,128)(2,1)} %reshape_reshape.8) | copy-start | bytes 688132
  149.1 21.8 %collective-permute-start.3 = (bf16[256,256]{1,0:T(8,128)(2,1)}, bf16[256,256]{1,0:T(8,128)(2,1)}, u32[]{:S(2)}, u32[]{:S(2)}) collective-permute-start(bf16[256,256]{1,0:T(8,128)(2,1)} %copy.65), channel_id=1, source_target_pairs={{8,0},{16,8},{24,16},{32,24},{40,32},{48,40},{56,48},{64,56},{72,6... | collective-permute-start | bytes 393224 | tf_op jit(solution)/shard_map/ppermute | solution.py:13
  152.3 8.0 %copy-start.2 = (f32[7,2,64,256]{3,2,1,0:T(8,128)}, f32[7,2,64,256]{3,2,1,0:T(8,128)S(1)}, u32[]{:S(2)}) copy-start(f32[7,2,64,256]{3,2,1,0:T(8,128)S(1)} %fusion.14) | copy-start | bytes 2752516
  160.3 3.3 %copy-start.5 = (f32[7,256,2,128]{1,3,2,0:T(8,128)S(1)}, f32[7,256,2,128]{1,3,2,0:T(8,128)}, u32[]{:S(2)}) copy-start(f32[7,256,2,128]{1,3,2,0:T(8,128)} %convolution_bitcast_fusion.1) | copy-start | bytes 5505028
  168.9 6.3 %collective-permute-start.2 = (bf16[256,256]{1,0:T(8,128)(2,1)S(1)}, bf16[256,256]{1,0:T(8,128)(2,1)S(1)}, u32[]{:S(2)}, u32[]{:S(2)}) collective-permute-start(bf16[256,256]{1,0:T(8,128)(2,1)S(1)} %copy.61), channel_id=1, source_target_pairs={{8,0},{16,8},{24,16},{32,24},{40,32},{48,40},{56,48},{64,56},{72,6... | collective-permute-start | bytes 393224 | tf_op jit(solution)/shard_map/ppermute | solution.py:13
  238.8 7.2 %copy-start.10 = (s32[1,64,1]{1,2,0:T(1,128)S(1)}, s32[1,64,1]{1,2,0:T(1,128)}, u32[]{:S(2)}) copy-start(s32[1,64,1]{1,2,0:T(1,128)} %param.19) | copy-start | bytes 772
  238.8 7.4 %copy-start.15 = (f32[7,2,64]{2,1,0:T(2,128)S(1)}, f32[7,2,64]{2,1,0:T(2,128)}, u32[]{:S(2)}) copy-start(f32[7,2,64]{2,1,0:T(2,128)} %copy-done.14) | copy-start | bytes 10756
  238.8 56.8 %all-to-all-start.2 = ((bf16[64,64,256]{2,1,0:T(8,128)(2,1)}), bf16[64,64,256]{2,1,0:T(8,128)(2,1)S(1)}, u32[]{:S(2)}, u32[]{:S(2)}) async-start(bf16[64,64,256]{2,1,0:T(8,128)(2,1)} %get-tuple-element.35), calls=%async_computation.2 | async-start | bytes 4194304 | tf_op jit(solution)/shard_map/all_to_all | solution.py:141
where the time goes:
time: 302 us; the launch traced here: 300 us
  blocking collectives  119 us (39%)
  waiting for transfers between devices  82.8 us (27%)
  local copies, waits for them, and re-layouts  34 us (11%)
  starting transfers between devices  26 us (9%)
  matrix products  21.4 us (7%)
  other arithmetic  15.5 us (5%)
    all_to_all x1, blocking collectives, local(): lax.all_to_all(key_send, 'seq', split_axis=0, concat_axis=0, tiled=True)  61.2 us
    all_to_all x1, blocking collectives, local(): lax.all_to_all(value_return, 'seq', split_axis=0, concat_axis=0, tiled=True)  58 us
    all_to_all x1, waiting for transfers between devices, local(): lax.all_to_all(value_send, 'seq', split_axis=0, concat_axis=0, tiled=True)  45.5 us
    all_to_all x1, waiting for transfers between devices, local(): lax.all_to_all(key_return, 'seq', split_axis=0, concat_axis=0, tiled=True)  35.5 us
    ppermute x4, starting transfers between devices, from_behind(): lax.ppermute(value, axis, [(source, source + steps) for source in range(f...  11.7 us
    dot_general x1, matrix products, backward_blocks(): jnp.einsum('bhqk,bqhd->bkhd', grad_scores, query_heads, preferred_element...  8 us
    all_to_all x1, starting transfers between devices, local(): lax.all_to_all(key_return, 'seq', split_axis=0, concat_axis=0, tiled=True)  7.16 us
    all_to_all x1, starting transfers between devices, local(): lax.all_to_all(value_send, 'seq', split_axis=0, concat_axis=0, tiled=True)  7.15 us
  transfers between devices with their start and end apart: 6, of which 4 were waited for; matrix products, arithmetic and copies ran while one was open for 14% of the time, Pallas kernels for 0%

commit v1 on v0

v1 whole, which is shorter than its diff:
```python
import functools

import jax
import jax.numpy as jnp
from jax import lax
from jax.experimental import pallas as pl
from jax.experimental.pallas import tpu as pltpu
from jax.sharding import PartitionSpec as P

HEAD_DIM = 128
GROUP = 64
VMEM_LIMIT = 24 * 1024 * 1024
SCALE = HEAD_DIM ** (-0.5)

VM = pl.BlockSpec(memory_space=pltpu.VMEM)
SM = pl.BlockSpec(memory_space=pltpu.SMEM)


def call(kernel, out_shape, n_smem, n_vmem, flops=0, moved=0, scratch=()):
    return pl.pallas_call(
        kernel,
        out_shape=out_shape,
        in_specs=[SM] * n_smem + [VM] * n_vmem,
        out_specs=jax.tree.map(lambda _: VM, out_shape),
        scratch_shapes=list(scratch),
        compiler_params=pltpu.CompilerParams(vmem_limit_bytes=VMEM_LIMIT),
        cost_estimate=pl.CostEstimate(flops=flops, bytes_accessed=moved, transcendentals=0),
    )


def pack_kernel(table, units, slots):
    def body(slot, carry):
        unit = table[slot]

        @pl.when(unit >= 0)
        def _():
            slots[slot] = units[unit]

        @pl.when(unit < 0)
        def _():
            slots[slot] = jnp.zeros(slots.shape[1:], slots.dtype)

        return carry

    lax.fori_loop(0, slots.shape[0], body, 0)


def unpack_kernel(table, slots, units):
    units[...] = jnp.zeros(units.shape, units.dtype)

    def body(slot, carry):
        unit = table[slot]

        @pl.when(unit >= 0)
        def _():
            units[unit] = slots[slot]

        return carry

    lax.fori_loop(0, slots.shape[0], body, 0)


def dot(a, b, contract):
    return lax.dot_general(a, b, ((contract[:1], contract[1:]), ((), ())), preferred_element_type=jnp.float32)


def gather_group(source, slots, group, per_group):
    return jnp.concatenate([slots[source[group * per_group + j]] for j in range(per_group)], axis=0)


def scatter_group(source, slots, group, per_group, column, part):
    for j in range(per_group):
        slots[source[group * per_group + j], :, column] = part[j * GROUP : (j + 1) * GROUP]


def probs_kernel(per_group, source, queries, grads, keys, probs, value_send):
    value_send[...] = jnp.zeros(value_send.shape, value_send.dtype)

    def body(group, carry):
        rows = pl.ds(pl.multiple_of(group * GROUP, GROUP), GROUP)
        key_block = gather_group(source, keys, group, per_group)
        for head in range(queries.shape[1] // HEAD_DIM):
            column = slice(head * HEAD_DIM, (head + 1) * HEAD_DIM)
            scores = dot(queries[rows, column], key_block[:, column], (1, 1)) * SCALE
            powers = jnp.exp(scores - jnp.max(scores, axis=-1, keepdims=True))
            chances = powers / jnp.sum(powers, axis=-1, keepdims=True)
            probs[group, head] = chances
            value_part = dot(chances.astype(jnp.bfloat16), grads[rows, column], (0, 0))
            scatter_group(source, value_send, group, per_group, column, value_part.astype(jnp.bfloat16))
        return carry

    lax.fori_loop(0, probs.shape[0], body, 0)


def grads_kernel(per_group, source, queries, grads, probs, keys, values, attended, query_grad, key_send):
    key_send[...] = jnp.zeros(key_send.shape, key_send.dtype)

    def body(group, carry):
        rows = pl.ds(pl.multiple_of(group * GROUP, GROUP), GROUP)
        key_block = gather_group(source, keys, group, per_group)
        value_block = gather_group(source, values, group, per_group)
        for head in range(queries.shape[1] // HEAD_DIM):
            column = slice(head * HEAD_DIM, (head + 1) * HEAD_DIM)
            chances = probs[group, head]
            mixed = dot(chances.astype(jnp.bfloat16), value_block[:, column], (1, 0))
            attended[rows, column] = mixed.astype(jnp.bfloat16)
            grad_probs = dot(grads[rows, column], value_block[:, column], (1, 1))
            row_dot = jnp.sum(chances * grad_probs, axis=-1, keepdims=True)
            grad_scores = (chances * (grad_probs - row_dot) * SCALE).astype(jnp.bfloat16)
            query_part = dot(grad_scores, key_block[:, column], (1, 0))
            query_grad[rows, column] = query_part.astype(jnp.bfloat16)
            key_part = dot(grad_scores, queries[rows, column], (0, 0))
            scatter_group(source, key_send, group, per_group, column, key_part.astype(jnp.bfloat16))
        return carry

    lax.fori_loop(0, probs.shape[0], body, 0)


def shift(value, axis, steps):
    count = lax.axis_size(axis)
    first, last = max(0, -steps), min(count, count - steps)
    return lax.ppermute(value, axis, [(at, at + steps) for at in range(first, last)])


def exchange(slots):
    return lax.all_to_all(slots, "seq", split_axis=0, concat_axis=0, tiled=True)


def local(queries, neighbor_keys, neighbor_values, out_grad, neighbor_source, send_unit):
    tok_rows, cols = queries.shape
    groups, per_group = neighbor_source.shape
    units = neighbor_keys.shape[0] // GROUP
    slots = send_unit.shape[1] * send_unit.shape[2]
    heads = cols // HEAD_DIM
    low = jnp.bfloat16
    table = send_unit.reshape(slots)
    source = neighbor_source.reshape(units)
    slot_shape = jax.ShapeDtypeStruct((slots, GROUP, cols), low)
    unit_shape = jax.ShapeDtypeStruct((units, GROUP, cols), low)
    tok_shape = jax.ShapeDtypeStruct((tok_rows, cols), low)
    slot_bytes = slots * GROUP * cols * 2
    pack = call(pack_kernel, slot_shape, 1, 1, moved=2 * slot_bytes)
    unpack = call(unpack_kernel, unit_shape, 1, 1, moved=2 * slot_bytes)
    matmul = 2 * tok_rows * cols * per_group * GROUP

    key_slots = exchange(pack(table, neighbor_keys.reshape(unit_shape.shape)))
    value_slots = exchange(pack(table, neighbor_values.reshape(unit_shape.shape)))

    edge = GROUP - 1
    ahead = shift(jnp.stack([queries[:GROUP], out_grad[:GROUP]]), "seq", -1)
    group_queries = jnp.concatenate([queries[edge:], ahead[0, :edge]], axis=0)
    group_grads = jnp.concatenate([out_grad[edge:], ahead[1, :edge]], axis=0)

    probs, value_send = call(
        functools.partial(probs_kernel, per_group),
        (jax.ShapeDtypeStruct((groups, heads, GROUP, per_group * GROUP), jnp.float32), slot_shape),
        1, 3, flops=2 * matmul, moved=2 * slot_bytes,
    )(source, group_queries, group_grads, key_slots)
    value_back = exchange(value_send)
    mixed, query_part, key_send = call(
        functools.partial(grads_kernel, per_group),
        (tok_shape, tok_shape, slot_shape),
        1, 5, flops=4 * matmul, moved=3 * slot_bytes,
    )(source, group_queries, group_grads, probs, key_slots, value_slots)
    key_back = exchange(key_send)

    behind = shift(jnp.stack([mixed[-GROUP:], query_part[-GROUP:]]), "seq", 1)
    attended = jnp.concatenate([behind[0, 1:], mixed[: tok_rows - edge]], axis=0)
    query_grad = jnp.concatenate([behind[1, 1:], query_part[: tok_rows - edge]], axis=0)
    value_grad = unpack(table, value_back).reshape(units * GROUP, cols)
    key_grad = unpack(table, key_back).reshape(units * GROUP, cols)
    return (attended, query_grad, key_grad, value_grad)


def solution(mesh):
    return jax.shard_map(
        local,
        mesh=mesh,
        in_specs=(
            P("seq", "mp"),
            P("seq", "mp"),
            P("seq", "mp"),
            P("seq", "mp"),
            P("seq", None),
            P("seq", None, None),
        ),
        out_specs=(P("seq", "mp"), P("seq", "mp"), P("seq", "mp"), P("seq", "mp")),
        check_vma=False,
    )
```

time: 302 us -> 258 us (0.85)
  blocking collectives: 119 us -> 63.8 us
  waiting for transfers between devices: 82.8 us -> 129 us
  local copies, waits for them, and re-layouts: 34 us -> 7.67 us
  matrix products: 21.4 us -> 0 us
  Pallas kernels: 0 us -> 20.5 us
  other arithmetic: 15.5 us -> 1.49 us
  starting transfers between devices: 26 us -> 32.1 us
    all_to_all x2 -> x1, blocking collectives: 119 us -> 63.8 us  [exchange(): return lax.all_to_all(slots, 'seq', split_axis=0, concat_axis=0, tiled=True)]
    all_to_all x2 -> x3, waiting for transfers between devices: 80.9 us -> 120 us  [exchange(): return lax.all_to_all(slots, 'seq', split_axis=0, concat_axis=0, tiled=True)]
    pallas_call x0 -> x6, Pallas kernels: none -> 20.5 us  [the longest x1 6.16 us: local(): call(functools.partial(grads_kernel, per_group), (tok_shape, tok_shape, s...]
    dot_general x5 -> x0, matrix products: 18.9 us -> none  [the longest x1 8 us: backward_blocks(): jnp.einsum('bhqk,bqhd->bkhd', grad_scores, query_heads, preferred_element...]
    gather x8 -> x0, local copies, waits for them, and re-layouts: 17 us -> none  [the longest x2 4.6 us: arrange_slots(): picked = jnp.take(received, source_flat, axis=0)]
    select_n x9 -> x0, other arithmetic: 12 us -> none  [the longest x1 3.57 us: local(): jnp.where(slot_used, jnp.take(value_grad_units, slot_which, axis=0), zero...]
    all_to_all x2 -> x3, starting transfers between devices: 14.3 us -> 26.1 us  [exchange(): return lax.all_to_all(slots, 'seq', split_axis=0, concat_axis=0, tiled=True)]
    ppermute x4 -> x2, waiting for transfers between devices: 1.83 us -> 8.14 us  [shift(): lax.ppermute(value, axis, [(at, at + steps) for at in range(first, last)])]
  transfers between devices with their start and end apart: 6 -> 5, of which waited for: 4 -> 5; matrix products, arithmetic and copies ran while one was open for 14% -> 1% of each run, Pallas kernels for 0% -> 4%
where the time goes in v1:
time: 258 us; the launch traced here: 255 us
  waiting for transfers between devices  129 us (50%)
  blocking collectives  63.8 us (25%)
  starting transfers between devices  32.1 us (12%)
  Pallas kernels  20.5 us (8%)
  local copies, waits for them, and re-layouts  7.67 us (3%)
    all_to_all x3, waiting for transfers between devices, exchange(): return lax.all_to_all(slots, 'seq', split_axis=0, concat_axis=0, tiled=True)  120 us
    all_to_all x1, blocking collectives, exchange(): return lax.all_to_all(slots, 'seq', split_axis=0, concat_axis=0, tiled=True)  63.8 us
    all_to_all x3, starting transfers between devices, exchange(): return lax.all_to_all(slots, 'seq', split_axis=0, concat_axis=0, tiled=True)  26.1 us
    ppermute x2, waiting for transfers between devices, shift(): lax.ppermute(value, axis, [(at, at + steps) for at in range(first, last)])  8.14 us
    unnamed x27, local copies, waits for them, and re-layouts  7.44 us
    pallas_call x1, Pallas kernels, local(): call(functools.partial(grads_kernel, per_group), (tok_shape, tok_shape, s...  6.16 us
    pallas_call x1, Pallas kernels, local(): call(functools.partial(probs_kernel, per_group), (jax.ShapeDtypeStruct((g...  6.09 us
    ppermute x2, starting transfers between devices, shift(): lax.ppermute(value, axis, [(at, at + steps) for at in range(first, last)])  5.98 us
  transfers between devices with their start and end apart: 5, of which 5 were waited for; matrix products, arithmetic and copies ran while one was open for 1% of the time, Pallas kernels for 4%

profile of v1, /device:TPU:1, one launch (start us, length us, event | category | flops | bytes accessed | tf_op | source)
XLA Modules:
  0.0 254.9 jit_solution(3095409355316718808)
XLA Ops:
  0.6 1.1 copy-done.4
  2.4 1.7 shard_map.93
  4.2 1.3 copy-done.2
  5.5 11.8 %all-to-all-start = ((bf16[64,64,256]{2,1,0:T(8,128)(2,1)}), bf16[64,64,256]{2,1,0:T(8,128)(2,1)S(1)}, u32[]{:S(2)}, u32[]{:S(2)}) async-start(bf16[64,64,256]{2,1,0:T(8,128)(2,1)} %copy-done.2), calls=%async_computation | async-start | bytes 4194304 | tf_op jit(solution)/shard_map/all_to_all | solution.py:126
  17.3 1.7 shard_map.95
  19.0 1.3 copy-done
  20.3 46.6 %all-to-all-done.keys = bf16[64,64,256]{2,1,0:T(8,128)(2,1)S(1)} async-done(((bf16[64,64,256]{2,1,0:T(8,128)(2,1)}), bf16[64,64,256]{2,1,0:T(8,128)(2,1)S(1)}, u32[]{:S(2)}, u32[]{:S(2)}) %all-to-all-start) | async-done | bytes 2097184 | tf_op jit(solution)/shard_map/all_to_all | solution.py:126
  66.9 7.2 %all-to-all-start.1 = ((bf16[64,64,256]{2,1,0:T(8,128)(2,1)}), bf16[64,64,256]{2,1,0:T(8,128)(2,1)}, u32[]{:S(2)}, u32[]{:S(2)}) async-start(bf16[64,64,256]{2,1,0:T(8,128)(2,1)} %copy-done), calls=%async_computation.1 | async-start | bytes 4194304 | tf_op jit(solution)/shard_map/all_to_all | solution.py:126
  74.2 2.4 collective-permute-start
  76.9 5.9 %collective-permute-done = bf16[2,64,256]{2,1,0:T(8,128)(2,1)S(1)} collective-permute-done((bf16[2,64,256]{2,1,0:T(8,128)(2,1)S(1)}, bf16[2,64,256]{2,1,0:T(8,128)(2,1)S(1)}, u32[]{:S(2)}, u32[]{:S(2)}) %collective-permute-start) | collective-permute-done | bytes 65568 | tf_op jit(solution)/shard_map/ppermute | solution.py:122
  82.9 6.1 %shard_map.94 = (f32[6,2,64,256]{3,2,1,0:T(8,128)S(1)}, bf16[64,64,256]{2,1,0:T(8,128)(2,1)S(1)}) custom-call(s32[24]{0:T(128)S(1)} %reshape.26.source, bf16[384,256]{1,0:T(8,128)(2,1)S(1)} %pad_maximum_fusion.queries, bf16[384,256]{1,0:T(8,128)(2,1)S(1)} %pad_maximum_fusion.1.grads, bf16[64,64,256]{2,1,0:T(8,128)(2,1)S(1)} %all-to-all-done.keys), custom_call_target="tpu_custom_call" | custom-call | flops 100663296 | bytes 4194304 | tf_op jit(solution)/shard_map/pallas_call | solution.py:154
  89.0 1.3 copy-done.3
  90.3 33.4 %all-to-all-done.1.values = bf16[64,64,256]{2,1,0:T(8,128)(2,1)} async-done(((bf16[64,64,256]{2,1,0:T(8,128)(2,1)}), bf16[64,64,256]{2,1,0:T(8,128)(2,1)}, u32[]{:S(2)}, u32[]{:S(2)}) %all-to-all-start.1) | async-done | bytes 2097184 | tf_op jit(solution)/shard_map/all_to_all | solution.py:126
  123.7 6.2 %shard_map.96 = (bf16[384,256]{1,0:T(8,128)(2,1)S(1)}, bf16[384,256]{1,0:T(8,128)(2,1)S(1)}, bf16[64,64,256]{2,1,0:T(8,128)(2,1)S(1)}) custom-call(s32[24]{0:T(128)S(1)} %reshape.26.source, bf16[384,256]{1,0:T(8,128)(2,1)S(1)} %pad_maximum_fusion.queries, bf16[384,256]{1,0:T(8,128)(2,1)S(1)} %pad_maximum_fusion.1.grads, ...), custom_call_target="tpu_custom_call" | custom-call | flops 201326592 | bytes 6291456 | tf_op jit(solution)/shard_map/pallas_call | solution.py:160
  129.9 63.8 %all_to_all.20.slots = bf16[64,64,256]{2,1,0:T(8,128)(2,1)} all-to-all(bf16[64,64,256]{2,1,0:T(8,128)(2,1)S(1)} %get-tuple-element.12), channel_id=1, replica_groups=mesh['seq'=64,'mp'=8] {'seq'}, dimensions={0} | all-to-all | bytes 4194304 | tf_op jit(solution)/shard_map/all_to_all | solution.py:126
  193.7 7.1 %all-to-all-start.3 = ((bf16[64,64,256]{2,1,0:T(8,128)(2,1)}), bf16[64,64,256]{2,1,0:T(8,128)(2,1)S(1)}, u32[]{:S(2)}, u32[]{:S(2)}) async-start(bf16[64,64,256]{2,1,0:T(8,128)(2,1)} %copy-done.3), calls=%async_computation.3 | async-start | bytes 4194304 | tf_op jit(solution)/shard_map/all_to_all | solution.py:126
  200.9 3.5 %collective-permute-start.1 = (bf16[2,64,256]{2,1,0:T(8,128)(2,1)S(1)}, bf16[2,64,256]{2,1,0:T(8,128)(2,1)S(1)}, u32[]{:S(2)}, u32[]{:S(2)}) collective-permute-start(bf16[2,64,256]{2,1,0:T(8,128)(2,1)S(1)} %pad_maximum_fusion.5), channel_id=1, source_target_pairs={{0,8},{8,16},{16,24},{24,32},{32,40},{40,48},{48,56},{56,64},{64,7... | collective-permute-start | bytes 196616 | tf_op jit(solution)/shard_map/ppermute | solution.py:122
  204.5 2.2 collective-permute-done.1
  206.8 0.7 pad_maximum_fusion.3
  207.5 0.7 pad_maximum_fusion.2
  208.2 1.6 copy-done.1
  209.8 2.4 shard_map.97
  212.2 40.4 %all-to-all-done.3.slots = bf16[64,64,256]{2,1,0:T(8,128)(2,1)S(1)} async-done(((bf16[64,64,256]{2,1,0:T(8,128)(2,1)}), bf16[64,64,256]{2,1,0:T(8,128)(2,1)S(1)}, u32[]{:S(2)}, u32[]{:S(2)}) %all-to-all-start.3) | async-done | bytes 2097184 | tf_op jit(solution)/shard_map/all_to_all | solution.py:126
  252.5 2.4 shard_map.98
  (36 shorter events, 1.1 us)
Async XLA Ops:
  0.6 1.1 copy-start.4
  1.8 0.7 copy-start.8
  4.2 1.3 copy-start.2
  5.5 11.8 %copy-start.5 = (bf16[1536,256]{1,0:T(8,128)(2,1)S(1)}, bf16[1536,256]{1,0:T(8,128)(2,1)}, u32[]{:S(2)}) copy-start(bf16[1536,256]{1,0:T(8,128)(2,1)} %param.8) | copy-start | bytes 2359300
  5.5 11.8 %copy-start.9 = (s32[1,64,1]{1,2,0:T(1,128)S(1)}, s32[1,64,1]{1,2,0:T(1,128)}, u32[]{:S(2)}) copy-start(s32[1,64,1]{1,2,0:T(1,128)} %param.11) | copy-start | bytes 772
  5.5 61.4 %all-to-all-start = ((bf16[64,64,256]{2,1,0:T(8,128)(2,1)}), bf16[64,64,256]{2,1,0:T(8,128)(2,1)S(1)}, u32[]{:S(2)}, u32[]{:S(2)}) async-start(bf16[64,64,256]{2,1,0:T(8,128)(2,1)} %copy-done.2), calls=%async_computation | async-start | bytes 4194304 | tf_op jit(solution)/shard_map/all_to_all | solution.py:126
  19.0 1.3 copy-start
  20.3 53.8 %copy-start.10 = (bf16[384,256]{1,0:T(8,128)(2,1)S(1)}, bf16[384,256]{1,0:T(8,128)(2,1)}, u32[]{:S(2)}) copy-start(bf16[384,256]{1,0:T(8,128)(2,1)} %param.6) | copy-start | bytes 589828
  20.3 53.8 %copy-start.11 = (bf16[384,256]{1,0:T(8,128)(2,1)S(1)}, bf16[384,256]{1,0:T(8,128)(2,1)}, u32[]{:S(2)}) copy-start(bf16[384,256]{1,0:T(8,128)(2,1)} %param.9) | copy-start | bytes 589828
  20.3 56.4 %copy-start.12 = (s32[6,4]{0,1:T(4,128)S(1)}, s32[6,4]{0,1:T(4,128)}, u32[]{:S(2)}) copy-start(s32[6,4]{0,1:T(4,128)} %param.10) | copy-start | bytes 292
  66.9 56.8 %all-to-all-start.1 = ((bf16[64,64,256]{2,1,0:T(8,128)(2,1)}), bf16[64,64,256]{2,1,0:T(8,128)(2,1)}, u32[]{:S(2)}, u32[]{:S(2)}) async-start(bf16[64,64,256]{2,1,0:T(8,128)(2,1)} %copy-done), calls=%async_computation.1 | async-start | bytes 4194304 | tf_op jit(solution)/shard_map/all_to_all | solution.py:126
  74.2 8.6 %collective-permute-start = (bf16[2,64,256]{2,1,0:T(8,128)(2,1)S(1)}, bf16[2,64,256]{2,1,0:T(8,128)(2,1)S(1)}, u32[]{:S(2)}, u32[]{:S(2)}) collective-permute-start(bf16[2,64,256]{2,1,0:T(8,128)(2,1)S(1)} %pad_maximum_fusion.4), channel_id=1, source_target_pairs={{8,0},{16,8},{24,16},{32,24},{40,32},{48,40},{56,48},{64,56},{72,6... | collective-permute-start | bytes 196616 | tf_op jit(solution)/shard_map/ppermute | solution.py:122
  89.0 1.3 copy-start.3
  129.9 63.8 %copy-start.6 = (bf16[384,256]{1,0:T(8,128)(2,1)}, bf16[384,256]{1,0:T(8,128)(2,1)S(1)}, u32[]{:S(2)}) copy-start(bf16[384,256]{1,0:T(8,128)(2,1)S(1)} %get-tuple-element.10) | copy-start | bytes 589828
  193.7 7.2 %copy-start.7 = (bf16[384,256]{1,0:T(8,128)(2,1)S(1)}, bf16[384,256]{1,0:T(8,128)(2,1)}, u32[]{:S(2)}) copy-start(bf16[384,256]{1,0:T(8,128)(2,1)} %copy-done.6) | copy-start | bytes 589828
  193.7 58.8 %all-to-all-start.3 = ((bf16[64,64,256]{2,1,0:T(8,128)(2,1)}), bf16[64,64,256]{2,1,0:T(8,128)(2,1)S(1)}, u32[]{:S(2)}, u32[]{:S(2)}) async-start(bf16[64,64,256]{2,1,0:T(8,128)(2,1)} %copy-done.3), calls=%async_computation.3 | async-start | bytes 4194304 | tf_op jit(solution)/shard_map/all_to_all | solution.py:126
  200.9 5.8 %collective-permute-start.1 = (bf16[2,64,256]{2,1,0:T(8,128)(2,1)S(1)}, bf16[2,64,256]{2,1,0:T(8,128)(2,1)S(1)}, u32[]{:S(2)}, u32[]{:S(2)}) collective-permute-start(bf16[2,64,256]{2,1,0:T(8,128)(2,1)S(1)} %pad_maximum_fusion.5), channel_id=1, source_target_pairs={{0,8},{8,16},{16,24},{24,32},{32,40},{40,48},{48,56},{56,64},{64,7... | collective-permute-start | bytes 196616 | tf_op jit(solution)/shard_map/ppermute | solution.py:122
  208.2 1.6 copy-start.1

commit v2 on v1

v2 whole, which is shorter than its diff:
```python
import functools

import jax
import jax.numpy as jnp
from jax import lax
from jax.experimental import pallas as pl
from jax.experimental.pallas import tpu as pltpu
from jax.sharding import PartitionSpec as P

HEAD_DIM = 128
GROUP = 64
PAIR = 2 * GROUP
VMEM_LIMIT = 58 * 1024 * 1024
SCALE = HEAD_DIM ** (-0.5)

VM = pl.BlockSpec(memory_space=pltpu.VMEM)
SM = pl.BlockSpec(memory_space=pltpu.SMEM)
HB = pl.BlockSpec(memory_space=pltpu.HBM)


def call(kernel, in_specs, out_specs, out_shape, scratch=(), flops=0, moved=0):
    return pl.pallas_call(
        kernel,
        out_shape=out_shape,
        in_specs=in_specs,
        out_specs=out_specs,
        scratch_shapes=list(scratch),
        compiler_params=pltpu.CompilerParams(vmem_limit_bytes=VMEM_LIMIT),
        cost_estimate=pl.CostEstimate(flops=flops, bytes_accessed=moved, transcendentals=0),
    )


def pack_kernel(table, keys, values, slots, zeros, sem):
    zeros[...] = jnp.zeros(zeros.shape, zeros.dtype)

    def body(slot, carry):
        unit = table[slot]

        @pl.when(unit >= 0)
        def _():
            pltpu.make_async_copy(keys.at[unit], slots.at[slot, pl.ds(0, GROUP)], sem).start()
            pltpu.make_async_copy(values.at[unit], slots.at[slot, pl.ds(GROUP, GROUP)], sem).start()

        @pl.when(unit < 0)
        def _():
            pltpu.make_async_copy(zeros, slots.at[slot], sem).start()

        return carry

    lax.fori_loop(0, slots.shape[0], body, 0)
    pltpu.make_async_copy(slots, slots, sem).wait()


def unpack_kernel(which, slots, keys, values, zeros, key_sem, value_sem):
    zeros[...] = jnp.zeros(zeros.shape, zeros.dtype)

    def body(unit, carry):
        slot = which[unit]

        @pl.when(slot >= 0)
        def _():
            pltpu.make_async_copy(slots.at[slot, pl.ds(0, GROUP)], keys.at[unit], key_sem).start()
            pltpu.make_async_copy(slots.at[slot, pl.ds(GROUP, GROUP)], values.at[unit], value_sem).start()

        @pl.when(slot < 0)
        def _():
            pltpu.make_async_copy(zeros, keys.at[unit], key_sem).start()
            pltpu.make_async_copy(zeros, values.at[unit], value_sem).start()

        return carry

    lax.fori_loop(0, keys.shape[0], body, 0)
    pltpu.make_async_copy(keys, keys, key_sem).wait()
    pltpu.make_async_copy(values, values, value_sem).wait()


def dot(a, b, contract):
    return lax.dot_general(a, b, ((contract[:1], contract[1:]), ((), ())), preferred_element_type=jnp.float32)


def by_head(rows):
    blank = jnp.zeros((rows.shape[0], HEAD_DIM), rows.dtype)
    heads = rows.shape[1] // HEAD_DIM
    return jnp.concatenate(
        [
            jnp.concatenate(
                [rows[:, h * HEAD_DIM : (h + 1) * HEAD_DIM] if h == at else blank for h in range(heads)], axis=1
            )
            for at in range(heads)
        ],
        axis=0,
    )


def block_kernel(
    source, queries, grads, slots, send, probs, scores_grad, blocks, block_grads, zeros, in_sems, zero_sem, out_sem
):
    groups, per_group = blocks.shape[:2]
    keys, cols = per_group * GROUP, blocks.shape[3]
    low = jnp.bfloat16
    for group in range(groups):
        for j in range(per_group):
            slot = source[group * per_group + j]
            pltpu.make_async_copy(slots.at[slot], blocks.at[group, j], in_sems.at[group]).start()
    zeros[...] = jnp.zeros(zeros.shape, low)
    many = zeros.shape[0]
    for first in range(0, send.shape[0], many):
        pltpu.make_async_copy(zeros, send.at[pl.ds(first, many)], zero_sem).start()
    for group in range(groups):
        pltpu.make_async_copy(blocks.at[group], blocks.at[group], in_sems.at[group]).wait()
        rows = slice(group * GROUP, (group + 1) * GROUP)
        query = by_head(queries[rows])
        grad = by_head(grads[rows])
        key = blocks[group, :, :GROUP].reshape(keys, cols)
        value = blocks[group, :, GROUP:].reshape(keys, cols)
        scores = dot(key, query, (1, 1)) * SCALE
        powers = jnp.exp(scores - jnp.max(scores, axis=0, keepdims=True))
        chances = powers * (1.0 / jnp.sum(powers, axis=0, keepdims=True))
        chances_low = chances.astype(low)
        probs[group] = chances_low
        value_part = dot(chances_low, grad, (1, 0)).astype(low)
        block_grads[group, :, GROUP:] = value_part.reshape(per_group, GROUP, cols)
        grad_probs = dot(value, grad, (1, 1))
        row_dot = jnp.sum(chances * grad_probs, axis=0, keepdims=True)
        grad_low = (chances * (grad_probs - row_dot) * SCALE).astype(low)
        scores_grad[group] = grad_low
        key_part = dot(grad_low, query, (1, 0)).astype(low)
        block_grads[group, :, :GROUP] = key_part.reshape(per_group, GROUP, cols)
        if group == 0:
            pltpu.make_async_copy(send, send, zero_sem).wait()
        for j in range(per_group):
            slot = source[group * per_group + j]
            pltpu.make_async_copy(block_grads.at[group, j], send.at[slot], out_sem).start()
    pltpu.make_async_copy(block_grads, block_grads, out_sem).wait()


def token_kernel(source, probs, scores_grad, slots, attended, query_grad, blocks, in_sems):
    groups, per_group = blocks.shape[:2]
    keys, cols = per_group * GROUP, blocks.shape[3]
    for group in range(groups):
        for j in range(per_group):
            slot = source[group * per_group + j]
            pltpu.make_async_copy(slots.at[slot], blocks.at[group, j], in_sems.at[group]).start()
    for group in range(groups):
        pltpu.make_async_copy(blocks.at[group], blocks.at[group], in_sems.at[group]).wait()
        rows = slice(group * GROUP, (group + 1) * GROUP)
        key = blocks[group, :, :GROUP].reshape(keys, cols)
        value = blocks[group, :, GROUP:].reshape(keys, cols)
        mixed = dot(probs[group], value, (0, 0)).astype(jnp.bfloat16)
        query_part = dot(scores_grad[group], key, (0, 0)).astype(jnp.bfloat16)
        for head in range(cols // HEAD_DIM):
            own = slice(head * GROUP, (head + 1) * GROUP)
            column = slice(head * HEAD_DIM, (head + 1) * HEAD_DIM)
            attended[rows, column] = mixed[own, column]
            query_grad[rows, column] = query_part[own, column]


def shift(value, axis, steps):
    count = lax.axis_size(axis)
    first, last = max(0, -steps), min(count, count - steps)
    return lax.ppermute(value, axis, [(at, at + steps) for at in range(first, last)])


def exchange(slots):
    return lax.all_to_all(slots, "seq", split_axis=0, concat_axis=0, tiled=True)


def local(queries, neighbor_keys, neighbor_values, out_grad, neighbor_source, send_unit):
    tok_rows, cols = queries.shape
    groups, per_group = neighbor_source.shape
    units = neighbor_keys.shape[0] // GROUP
    slots = send_unit.shape[1] * send_unit.shape[2]
    heads, keys = cols // HEAD_DIM, per_group * GROUP
    low = jnp.bfloat16
    table = send_unit.reshape(slots)
    source = neighbor_source.reshape(units)
    slot_shape = jax.ShapeDtypeStruct((slots, PAIR, cols), low)
    unit_shape = jax.ShapeDtypeStruct((units, GROUP, cols), low)
    tok_shape = jax.ShapeDtypeStruct((tok_rows, cols), low)
    prob_shape = jax.ShapeDtypeStruct((groups, keys, heads * GROUP), low)
    slot_bytes = slots * PAIR * cols * 2
    matmul = 2 * groups * keys * heads * GROUP * cols
    blocks = pltpu.VMEM((groups, per_group, PAIR, cols), low)
    group_sems = pltpu.SemaphoreType.DMA((groups,))

    received = exchange(
        call(
            pack_kernel, [SM, HB, HB], HB, slot_shape,
            scratch=[pltpu.VMEM((PAIR, cols), low), pltpu.SemaphoreType.DMA],
            moved=2 * slot_bytes,
        )(table, neighbor_keys.reshape(unit_shape.shape), neighbor_values.reshape(unit_shape.shape))
    )

    edge = GROUP - 1
    ahead = shift(jnp.stack([queries[:GROUP], out_grad[:GROUP]]), "seq", -1)
    group_queries = jnp.concatenate([queries[edge:], ahead[0, :edge]], axis=0)
    group_grads = jnp.concatenate([out_grad[edge:], ahead[1, :edge]], axis=0)
    fills = table[None, :] == jnp.arange(units, dtype=jnp.int32)[:, None]
    which = jnp.max(jnp.where(fills, jnp.arange(slots, dtype=jnp.int32)[None, :], -1), axis=1)

    send, probs, scores_grad = call(
        block_kernel, [SM, VM, VM, HB], (HB, VM, VM), (slot_shape, prob_shape, prob_shape),
        scratch=[
            blocks, blocks, pltpu.VMEM((8, PAIR, cols), low),
            group_sems, pltpu.SemaphoreType.DMA, pltpu.SemaphoreType.DMA,
        ],
        flops=4 * matmul, moved=slot_bytes,
    )(source, group_queries, group_grads, received)
    returned = exchange(send)

    mixed, query_part = call(
        token_kernel, [SM, VM, VM, HB], (VM, VM), (tok_shape, tok_shape),
        scratch=[blocks, group_sems], flops=2 * matmul, moved=slot_bytes,
    )(source, probs, scores_grad, received)
    behind = shift(jnp.stack([mixed[-GROUP:], query_part[-GROUP:]]), "seq", 1)
    attended = jnp.concatenate([behind[0, 1:], mixed[: tok_rows - edge]], axis=0)
    query_grad = jnp.concatenate([behind[1, 1:], query_part[: tok_rows - edge]], axis=0)

    key_grad, value_grad = call(
        unpack_kernel, [SM, HB], (HB, HB), (unit_shape, unit_shape),
        scratch=[pltpu.VMEM((GROUP, cols), low), pltpu.SemaphoreType.DMA, pltpu.SemaphoreType.DMA],
        moved=slot_bytes,
    )(which, returned)
    flat = (units * GROUP, cols)
    return (attended, query_grad, key_grad.reshape(flat), value_grad.reshape(flat))


def solution(mesh):
    return jax.shard_map(
        local,
        mesh=mesh,
        in_specs=(
            P("seq", "mp"),
            P("seq", "mp"),
            P("seq", "mp"),
            P("seq", "mp"),
            P("seq", None),
            P("seq", None, None),
        ),
        out_specs=(P("seq", "mp"), P("seq", "mp"), P("seq", "mp"), P("seq", "mp")),
        check_vma=False,
    )
```

time: 258 us -> 318 us (1.23)
  Pallas kernels: 20.5 us -> 111 us
  blocking collectives: 63.8 us -> 0 us
  waiting for transfers between devices: 129 us -> 172 us
  starting transfers between devices: 32.1 us -> 26.4 us
  local copies, waits for them, and re-layouts: 7.67 us -> 4.22 us
    pallas_call x6 -> x4, Pallas kernels: 20.5 us -> 111 us  [the longest x1 49.4 us: local(): call(pack_kernel, [SM, HB, HB], HB, slot_shape, scratch=[pltpu.VMEM((PAIR...]
    all_to_all x1 -> x0, blocking collectives: 63.8 us -> none  [exchange(): return lax.all_to_all(slots, 'seq', split_axis=0, concat_axis=0, tiled=True)]
    all_to_all x3 -> x2, waiting for transfers between devices: 120 us -> 162 us  [exchange(): return lax.all_to_all(slots, 'seq', split_axis=0, concat_axis=0, tiled=True)]
    unnamed x27 -> x9, local copies, waits for them, and re-layouts: 7.44 us -> 0.12 us
    all_to_all x3 -> x2, starting transfers between devices: 26.1 us -> 20.3 us  [exchange(): return lax.all_to_all(slots, 'seq', split_axis=0, concat_axis=0, tiled=True)]
  transfers between devices with their start and end apart: 5 -> 4, of which waited for: 5 -> 3; matrix products, arithmetic and copies ran while one was open for 1% -> 2% of each run, Pallas kernels for 4% -> 1%
where the time goes in v2:
time: 318 us
  waiting for transfers between devices  172 us (54%)
  Pallas kernels  111 us (35%)
  starting transfers between devices  26.4 us (8%)
  local copies, waits for them, and re-layouts  4.22 us (1%)
  other arithmetic  3.48 us (1%)
    all_to_all x2, waiting for transfers between devices, exchange(): return lax.all_to_all(slots, 'seq', split_axis=0, concat_axis=0, tiled=True)  162 us
    pallas_call x1, Pallas kernels, local(): call(pack_kernel, [SM, HB, HB], HB, slot_shape, scratch=[pltpu.VMEM((PAIR...  49.4 us
    pallas_call x1, Pallas kernels, local(): call(unpack_kernel, [SM, HB], (HB, HB), (unit_shape, unit_shape), scratch...  49.4 us
    all_to_all x2, starting transfers between devices, exchange(): return lax.all_to_all(slots, 'seq', split_axis=0, concat_axis=0, tiled=True)  20.3 us
    ppermute x2, waiting for transfers between devices, shift(): lax.ppermute(value, axis, [(at, at + steps) for at in range(first, last)])  10.7 us
    pallas_call x1, Pallas kernels, local(): call(block_kernel, [SM, VM, VM, HB], (HB, VM, VM), (slot_shape, prob_shap...  7.44 us
  transfers between devices with their start and end apart: 4, of which 3 were waited for; matrix products, arithmetic and copies ran while one was open for 2% of the time, Pallas kernels for 1%

profile of v2, /device:TPU:1, one launch (start us, length us, event | category | flops | bytes accessed | tf_op | source)
XLA Modules:
  0.0 317.7 jit_solution(13079316361579917382)
XLA Ops:
  0.6 49.4 %shard_map.93 = bf16[64,128,256]{2,1,0:T(8,128)(2,1)} custom-call(s32[64]{0:T(128)} %bitcast.23, bf16[24,64,256]{2,1,0:T(8,128)(2,1)} %bitcast.21, bf16[24,64,256]{2,1,0:T(8,128)(2,1)} %bitcast.22), custom_call_target="tpu_custom_call" | custom-call | bytes 8388608 | tf_op jit(solution)/shard_map/pallas_call | solution.py:187
  50.1 0.0 copy-start.1
  50.1 0.0 copy-start.2
  50.1 12.0 %all-to-all-start = ((bf16[64,128,256]{2,1,0:T(8,128)(2,1)}), bf16[64,128,256]{2,1,0:T(8,128)(2,1)}, u32[]{:S(2)}, u32[]{:S(2)}) async-start(bf16[64,128,256]{2,1,0:T(8,128)(2,1)} %shard_map.93), calls=%async_computation | async-start | bytes 8388608 | tf_op jit(solution)/shard_map/all_to_all | solution.py:165
  62.2 2.5 collective-permute-start
  64.9 0.1 copy.12
  65.0 0.6 reshape.27.source
  65.6 10.7 %collective-permute-done = bf16[2,64,256]{2,1,0:T(8,128)(2,1)S(1)} collective-permute-done((bf16[2,64,256]{2,1,0:T(8,128)(2,1)S(1)}, bf16[2,64,256]{2,1,0:T(8,128)(2,1)S(1)}, u32[]{:S(2)}, u32[]{:S(2)}) %collective-permute-start) | collective-permute-done | bytes 65568 | tf_op jit(solution)/shard_map/ppermute | solution.py:161
  76.3 0.7 pad_maximum_fusion.queries
  77.0 0.7 pad_maximum_fusion.1.grads
  77.7 79.2 %all-to-all-done.slots = bf16[64,128,256]{2,1,0:T(8,128)(2,1)} async-done(((bf16[64,128,256]{2,1,0:T(8,128)(2,1)}), bf16[64,128,256]{2,1,0:T(8,128)(2,1)}, u32[]{:S(2)}, u32[]{:S(2)}) %all-to-all-start) | async-done | bytes 4194336 | tf_op jit(solution)/shard_map/all_to_all | solution.py:165
  156.8 7.4 %shard_map.94 = (bf16[64,128,256]{2,1,0:T(8,128)(2,1)}, bf16[6,256,128]{2,1,0:T(8,128)(2,1)}, bf16[6,256,128]{2,1,0:T(8,128)(2,1)}) custom-call(s32[24]{0:T(128)} %reshape.27.source, bf16[384,256]{1,0:T(8,128)(2,1)} %pad_maximum_fusion.queries, bf16[384,256]{1,0:T(8,128)(2,1)} %pad_maximum_fusion.1.grads, bf16[64,128,256]{2,1,0:T(8,128)(2,1)} %all-to-all-done.slots), custom_call_target="tpu_custom_call" | custom-call | flops 402653184 | bytes 4194304 | tf_op jit(solution)/shard_map/pallas_call | solution.py:201
  164.3 8.3 %all-to-all-start.1 = ((bf16[64,128,256]{2,1,0:T(8,128)(2,1)}), bf16[64,128,256]{2,1,0:T(8,128)(2,1)}, u32[]{:S(2)}, u32[]{:S(2)}) async-start(bf16[64,128,256]{2,1,0:T(8,128)(2,1)} %get-tuple-element.15), calls=%async_computation.1 | async-start | bytes 8388608 | tf_op jit(solution)/shard_map/all_to_all | solution.py:165
  172.6 4.2 %shard_map.95 = (bf16[384,256]{1,0:T(8,128)(2,1)}, bf16[384,256]{1,0:T(8,128)(2,1)}) custom-call(s32[24]{0:T(128)} %reshape.27.source, bf16[6,256,128]{2,1,0:T(8,128)(2,1)} %get-tuple-element.11.probs, bf16[6,256,128]{2,1,0:T(8,128)(2,1)} %get-tuple-element.12.scores_grad, bf16[64,128,256]{2,1,0:T(8,128)(2,1)} %all-to-all-done.slots), custom_call_target="tpu_custom_call" | custom-call | flops 201326592 | bytes 4194304 | tf_op jit(solution)/shard_map/pallas_call | solution.py:211
  176.8 0.8 slice_bitcast_fusion.4
  177.6 0.8 slice_bitcast_fusion.5
  178.4 3.5 %collective-permute-start.1 = (bf16[2,64,256]{2,1,0:T(8,128)(2,1)S(1)}, bf16[2,64,256]{2,1,0:T(8,128)(2,1)S(1)}, u32[]{:S(2)}, u32[]{:S(2)}) collective-permute-start(bf16[2,64,256]{2,1,0:T(8,128)(2,1)S(1)} %pad_maximum_fusion.5), channel_id=1, source_target_pairs={{0,8},{8,16},{16,24},{24,32},{32,40},{40,48},{48,56},{56,64},{64,7... | collective-permute-start | bytes 196616 | tf_op jit(solution)/shard_map/ppermute | solution.py:161
  181.9 0.6 select_reduce_fusion.which
  182.6 0.9 slice.47
  183.5 0.9 slice.45
  184.5 0.7 pad_maximum_fusion.3
  185.2 0.7 pad_maximum_fusion.2
  185.9 82.4 %all-to-all-done.1.slots = bf16[64,128,256]{2,1,0:T(8,128)(2,1)} async-done(((bf16[64,128,256]{2,1,0:T(8,128)(2,1)}), bf16[64,128,256]{2,1,0:T(8,128)(2,1)}, u32[]{:S(2)}, u32[]{:S(2)}) %all-to-all-start.1) | async-done | bytes 4194336 | tf_op jit(solution)/shard_map/all_to_all | solution.py:165
  268.3 49.4 %shard_map.96 = (bf16[24,64,256]{2,1,0:T(8,128)(2,1)}, bf16[24,64,256]{2,1,0:T(8,128)(2,1)}) custom-call(s32[24]{0:T(128)} %select_reduce_fusion.which, bf16[64,128,256]{2,1,0:T(8,128)(2,1)} %all-to-all-done.1.slots), custom_call_target="tpu_custom_call" | custom-call | bytes 4194304 | tf_op jit(solution)/shard_map/pallas_call | solution.py:219
  (14 shorter events, 0.2 us)
Async XLA Ops:
  50.1 12.1 %copy-start = (bf16[384,256]{1,0:T(8,128)(2,1)S(1)}, bf16[384,256]{1,0:T(8,128)(2,1)}, u32[]{:S(2)}) copy-start(bf16[384,256]{1,0:T(8,128)(2,1)} %param.6) | copy-start | bytes 589828
  50.1 12.1 %copy-start.1 = (bf16[384,256]{1,0:T(8,128)(2,1)S(1)}, bf16[384,256]{1,0:T(8,128)(2,1)}, u32[]{:S(2)}) copy-start(bf16[384,256]{1,0:T(8,128)(2,1)} %param.9) | copy-start | bytes 589828
  50.1 14.8 %copy-start.2 = (s32[6,4]{0,1:T(4,128)S(1)}, s32[6,4]{0,1:T(4,128)}, u32[]{:S(2)}) copy-start(s32[6,4]{0,1:T(4,128)} %param.10) | copy-start | bytes 292
  50.1 106.7 %all-to-all-start = ((bf16[64,128,256]{2,1,0:T(8,128)(2,1)}), bf16[64,128,256]{2,1,0:T(8,128)(2,1)}, u32[]{:S(2)}, u32[]{:S(2)}) async-start(bf16[64,128,256]{2,1,0:T(8,128)(2,1)} %shard_map.93), calls=%async_computation | async-start | bytes 8388608 | tf_op jit(solution)/shard_map/all_to_all | solution.py:165
  62.2 14.0 %collective-permute-start = (bf16[2,64,256]{2,1,0:T(8,128)(2,1)S(1)}, bf16[2,64,256]{2,1,0:T(8,128)(2,1)S(1)}, u32[]{:S(2)}, u32[]{:S(2)}) collective-permute-start(bf16[2,64,256]{2,1,0:T(8,128)(2,1)S(1)} %pad_maximum_fusion.4), channel_id=1, source_target_pairs={{8,0},{16,8},{24,16},{32,24},{40,32},{48,40},{56,48},{64,56},{72,6... | collective-permute-start | bytes 196616 | tf_op jit(solution)/shard_map/ppermute | solution.py:161
  164.3 104.0 %all-to-all-start.1 = ((bf16[64,128,256]{2,1,0:T(8,128)(2,1)}), bf16[64,128,256]{2,1,0:T(8,128)(2,1)}, u32[]{:S(2)}, u32[]{:S(2)}) async-start(bf16[64,128,256]{2,1,0:T(8,128)(2,1)} %get-tuple-element.15), calls=%async_computation.1 | async-start | bytes 8388608 | tf_op jit(solution)/shard_map/all_to_all | solution.py:165
  172.6 9.3 %copy-start.3 = (s32[1,64,1]{1,2,0:T(1,128)S(1)}, s32[1,64,1]{1,2,0:T(1,128)}, u32[]{:S(2)}) copy-start(s32[1,64,1]{1,2,0:T(1,128)} %param.11) | copy-start | bytes 772
  178.4 6.1 %collective-permute-start.1 = (bf16[2,64,256]{2,1,0:T(8,128)(2,1)S(1)}, bf16[2,64,256]{2,1,0:T(8,128)(2,1)S(1)}, u32[]{:S(2)}, u32[]{:S(2)}) collective-permute-start(bf16[2,64,256]{2,1,0:T(8,128)(2,1)S(1)} %pad_maximum_fusion.5), channel_id=1, source_target_pairs={{0,8},{8,16},{16,24},{24,32},{32,40},{40,48},{48,56},{56,64},{64,7... | collective-permute-start | bytes 196616 | tf_op jit(solution)/shard_map/ppermute | solution.py:161

commit v3 on v2

--- a/solution.py
+++ b/solution.py
@@ -30,46 +30,63 @@
     )
 
 
-def pack_kernel(table, keys, values, slots, zeros, sem):
+def pack_kernel(table, keys, values, slots, staged, zeros, in_sem, out_sem):
+    loads = [
+        pltpu.make_async_copy(keys, staged.at[:, pl.ds(0, GROUP)], in_sem.at[0]),
+        pltpu.make_async_copy(values, staged.at[:, pl.ds(GROUP, GROUP)], in_sem.at[1]),
+    ]
+    for load in loads:
+        load.start()
     zeros[...] = jnp.zeros(zeros.shape, zeros.dtype)
 
-    def body(slot, carry):
+    def blank(slot, carry):
+        @pl.when(table[slot] < 0)
+        def _():
+            pltpu.make_async_copy(zeros, slots.at[slot], out_sem).start()
+
+        return carry
+
+    def fill(slot, carry):
         unit = table[slot]
 
         @pl.when(unit >= 0)
         def _():
-            pltpu.make_async_copy(keys.at[unit], slots.at[slot, pl.ds(0, GROUP)], sem).start()
-            pltpu.make_async_copy(values.at[unit], slots.at[slot, pl.ds(GROUP, GROUP)], sem).start()
-
-        @pl.when(unit < 0)
-        def _():
-            pltpu.make_async_copy(zeros, slots.at[slot], sem).start()
+            pltpu.make_async_copy(staged.at[unit], slots.at[slot], out_sem).start()
 
         return carry
 
-    lax.fori_loop(0, slots.shape[0], body, 0)
-    pltpu.make_async_copy(slots, slots, sem).wait()
-
-
-def unpack_kernel(which, slots, keys, values, zeros, key_sem, value_sem):
+    lax.fori_loop(0, slots.shape[0], blank, 0)
+    for load in loads:
+        load.wait()
+    lax.fori_loop(0, slots.shape[0], fill, 0)
+    pltpu.make_async_copy(slots, slots, out_sem).wait()
+
+
+def unpack_kernel(which, slots, keys, values, staged, zeros, in_sems, key_sem, value_sem):
     zeros[...] = jnp.zeros(zeros.shape, zeros.dtype)
+    parts = in_sems.shape[0]
+    some = keys.shape[0] // parts
 
     def body(unit, carry):
         slot = which[unit]
+        sem = in_sems.at[unit // some]
 
         @pl.when(slot >= 0)
         def _():
-            pltpu.make_async_copy(slots.at[slot, pl.ds(0, GROUP)], keys.at[unit], key_sem).start()
-            pltpu.make_async_copy(slots.at[slot, pl.ds(GROUP, GROUP)], values.at[unit], value_sem).start()
+            pltpu.make_async_copy(slots.at[slot], staged.at[unit], sem).start()
 
         @pl.when(slot < 0)
         def _():
-            pltpu.make_async_copy(zeros, keys.at[unit], key_sem).start()
-            pltpu.make_async_copy(zeros, values.at[unit], value_sem).start()
+            pltpu.make_async_copy(zeros, staged.at[unit], sem).start()
 
         return carry
 
     lax.fori_loop(0, keys.shape[0], body, 0)
+    for part in range(parts):
+        own = pl.ds(part * some, some)
+        pltpu.make_async_copy(staged.at[own], staged.at[own], in_sems.at[part]).wait()
+        pltpu.make_async_copy(staged.at[own, pl.ds(0, GROUP)], keys.at[own], key_sem).start()
+        pltpu.make_async_copy(staged.at[own, pl.ds(GROUP, GROUP)], values.at[own], value_sem).start()
     pltpu.make_async_copy(keys, keys, key_sem).wait()
     pltpu.make_async_copy(values, values, value_sem).wait()
 
@@ -181,12 +198,16 @@
     slot_bytes = slots * PAIR * cols * 2
     matmul = 2 * groups * keys * heads * GROUP * cols
     blocks = pltpu.VMEM((groups, per_group, PAIR, cols), low)
+    staged = pltpu.VMEM((units, PAIR, cols), low)
     group_sems = pltpu.SemaphoreType.DMA((groups,))
 
     received = exchange(
         call(
             pack_kernel, [SM, HB, HB], HB, slot_shape,
-            scratch=[pltpu.VMEM((PAIR, cols), low), pltpu.SemaphoreType.DMA],
+            scratch=[
+                staged, pltpu.VMEM((PAIR, cols), low),
+                pltpu.SemaphoreType.DMA((2,)), pltpu.SemaphoreType.DMA,
+            ],
             moved=2 * slot_bytes,
         )(table, neighbor_keys.reshape(unit_shape.shape), neighbor_values.reshape(unit_shape.shape))
     )
@@ -218,7 +239,10 @@
 
     key_grad, value_grad = call(
         unpack_kernel, [SM, HB], (HB, HB), (unit_shape, unit_shape),
-        scratch=[pltpu.VMEM((GROUP, cols), low), pltpu.SemaphoreType.DMA, pltpu.SemaphoreType.DMA],
+        scratch=[
+            staged, pltpu.VMEM((PAIR, cols), low),
+            pltpu.SemaphoreType.DMA((4,)), pltpu.SemaphoreType.DMA, pltpu.SemaphoreType.DMA,
+        ],
         moved=slot_bytes,
     )(which, returned)
     flat = (units * GROUP, cols)

time: 318 us -> 227 us (0.71)
  Pallas kernels: 111 us -> 18.8 us
    pallas_call x1, Pallas kernels: 49.4 us -> 2.94 us  [local(): call(unpack_kernel, [SM, HB], (HB, HB), (unit_shape, unit_shape), scratch...]
    pallas_call x1, Pallas kernels: 49.4 us -> 4.19 us  [local(): call(pack_kernel, [SM, HB, HB], HB, slot_shape, scratch=[staged, pltpu.VM...]
  transfers between devices with their start and end apart: 4 -> 4, of which waited for: 3 -> 3; matrix products, arithmetic and copies ran while one was open for 2% -> 3% of each run, Pallas kernels for 1% -> 2%
where the time goes in v3:
time: 227 us; the launch traced here: 226 us
  waiting for transfers between devices  172 us (76%)
  starting transfers between devices  26.4 us (12%)
  Pallas kernels  18.8 us (8%)
  local copies, waits for them, and re-layouts  4.22 us (2%)
  other arithmetic  3.48 us (2%)
    all_to_all x2, waiting for transfers between devices, exchange(): return lax.all_to_all(slots, 'seq', split_axis=0, concat_axis=0, tiled=True)  162 us
    all_to_all x2, starting transfers between devices, exchange(): return lax.all_to_all(slots, 'seq', split_axis=0, concat_axis=0, tiled=True)  20.3 us
    ppermute x2, waiting for transfers between devices, shift(): lax.ppermute(value, axis, [(at, at + steps) for at in range(first, last)])  10.7 us
    pallas_call x1, Pallas kernels, local(): call(block_kernel, [SM, VM, VM, HB], (HB, VM, VM), (slot_shape, prob_shap...  7.44 us
    ppermute x2, starting transfers between devices, shift(): lax.ppermute(value, axis, [(at, at + steps) for at in range(first, last)])  6.09 us
  transfers between devices with their start and end apart: 4, of which 3 were waited for; matrix products, arithmetic and copies ran while one was open for 3% of the time, Pallas kernels for 2%

profile of v3, /device:TPU:1, one launch (start us, length us, event | category | flops | bytes accessed | tf_op | source)
XLA Modules:
  0.0 226.0 jit_solution(15192651326120876393)
XLA Ops:
  0.6 4.2 %shard_map.93 = bf16[64,128,256]{2,1,0:T(8,128)(2,1)} custom-call(s32[64]{0:T(128)} %bitcast.23, bf16[24,64,256]{2,1,0:T(8,128)(2,1)} %bitcast.21, bf16[24,64,256]{2,1,0:T(8,128)(2,1)} %bitcast.22), custom_call_target="tpu_custom_call" | custom-call | bytes 8388608 | tf_op jit(solution)/shard_map/pallas_call | solution.py:205
  4.8 0.0 copy-start.1
  4.9 0.0 copy-start.2
  4.9 12.0 %all-to-all-start = ((bf16[64,128,256]{2,1,0:T(8,128)(2,1)}), bf16[64,128,256]{2,1,0:T(8,128)(2,1)}, u32[]{:S(2)}, u32[]{:S(2)}) async-start(bf16[64,128,256]{2,1,0:T(8,128)(2,1)} %shard_map.93), calls=%async_computation | async-start | bytes 8388608 | tf_op jit(solution)/shard_map/all_to_all | solution.py:182
  17.0 2.5 %collective-permute-start = (bf16[2,64,256]{2,1,0:T(8,128)(2,1)S(1)}, bf16[2,64,256]{2,1,0:T(8,128)(2,1)S(1)}, u32[]{:S(2)}, u32[]{:S(2)}) collective-permute-start(bf16[2,64,256]{2,1,0:T(8,128)(2,1)S(1)} %pad_maximum_fusion.4), channel_id=1, source_target_pairs={{8,0},{16,8},{24,16},{32,24},{40,32},{48,40},{56,48},{64,56},{72,6... | collective-permute-start | bytes 196616 | tf_op jit(solution)/shard_map/ppermute | solution.py:178
  19.6 0.1 copy.12
  19.7 0.6 reshape.27.source
  20.3 10.7 %collective-permute-done = bf16[2,64,256]{2,1,0:T(8,128)(2,1)S(1)} collective-permute-done((bf16[2,64,256]{2,1,0:T(8,128)(2,1)S(1)}, bf16[2,64,256]{2,1,0:T(8,128)(2,1)S(1)}, u32[]{:S(2)}, u32[]{:S(2)}) %collective-permute-start) | collective-permute-done | bytes 65568 | tf_op jit(solution)/shard_map/ppermute | solution.py:178
  31.0 0.7 pad_maximum_fusion.queries
  31.7 0.7 pad_maximum_fusion.1.grads
  32.4 79.2 %all-to-all-done.slots = bf16[64,128,256]{2,1,0:T(8,128)(2,1)} async-done(((bf16[64,128,256]{2,1,0:T(8,128)(2,1)}), bf16[64,128,256]{2,1,0:T(8,128)(2,1)}, u32[]{:S(2)}, u32[]{:S(2)}) %all-to-all-start) | async-done | bytes 4194336 | tf_op jit(solution)/shard_map/all_to_all | solution.py:182
  111.6 7.4 %shard_map.94 = (bf16[64,128,256]{2,1,0:T(8,128)(2,1)}, bf16[6,256,128]{2,1,0:T(8,128)(2,1)}, bf16[6,256,128]{2,1,0:T(8,128)(2,1)}) custom-call(s32[24]{0:T(128)} %reshape.27.source, bf16[384,256]{1,0:T(8,128)(2,1)} %pad_maximum_fusion.queries, bf16[384,256]{1,0:T(8,128)(2,1)} %pad_maximum_fusion.1.grads, bf16[64,128,256]{2,1,0:T(8,128)(2,1)} %all-to-all-done.slots), custom_call_target="tpu_custom_call" | custom-call | flops 402653184 | bytes 4194304 | tf_op jit(solution)/shard_map/pallas_call | solution.py:222
  119.0 8.3 %all-to-all-start.1 = ((bf16[64,128,256]{2,1,0:T(8,128)(2,1)}), bf16[64,128,256]{2,1,0:T(8,128)(2,1)}, u32[]{:S(2)}, u32[]{:S(2)}) async-start(bf16[64,128,256]{2,1,0:T(8,128)(2,1)} %get-tuple-element.15), calls=%async_computation.1 | async-start | bytes 8388608 | tf_op jit(solution)/shard_map/all_to_all | solution.py:182
  127.3 4.2 %shard_map.95 = (bf16[384,256]{1,0:T(8,128)(2,1)}, bf16[384,256]{1,0:T(8,128)(2,1)}) custom-call(s32[24]{0:T(128)} %reshape.27.source, bf16[6,256,128]{2,1,0:T(8,128)(2,1)} %get-tuple-element.11.probs, bf16[6,256,128]{2,1,0:T(8,128)(2,1)} %get-tuple-element.12.scores_grad, bf16[64,128,256]{2,1,0:T(8,128)(2,1)} %all-to-all-done.slots), custom_call_target="tpu_custom_call" | custom-call | flops 201326592 | bytes 4194304 | tf_op jit(solution)/shard_map/pallas_call | solution.py:232
  131.6 0.8 slice_bitcast_fusion.4
  132.4 0.8 slice_bitcast_fusion.5
  133.1 3.5 %collective-permute-start.1 = (bf16[2,64,256]{2,1,0:T(8,128)(2,1)S(1)}, bf16[2,64,256]{2,1,0:T(8,128)(2,1)S(1)}, u32[]{:S(2)}, u32[]{:S(2)}) collective-permute-start(bf16[2,64,256]{2,1,0:T(8,128)(2,1)S(1)} %pad_maximum_fusion.5), channel_id=1, source_target_pairs={{0,8},{8,16},{16,24},{24,32},{32,40},{40,48},{48,56},{56,64},{64,7... | collective-permute-start | bytes 196616 | tf_op jit(solution)/shard_map/ppermute | solution.py:178
  136.7 0.6 select_reduce_fusion.which
  137.3 0.9 slice.47
  138.2 0.9 slice.45
  139.2 0.7 pad_maximum_fusion.3
  139.9 0.7 pad_maximum_fusion.2
  140.7 82.4 %all-to-all-done.1.slots = bf16[64,128,256]{2,1,0:T(8,128)(2,1)} async-done(((bf16[64,128,256]{2,1,0:T(8,128)(2,1)}), bf16[64,128,256]{2,1,0:T(8,128)(2,1)}, u32[]{:S(2)}, u32[]{:S(2)}) %all-to-all-start.1) | async-done | bytes 4194336 | tf_op jit(solution)/shard_map/all_to_all | solution.py:182
  223.1 2.9 %shard_map.96 = (bf16[24,64,256]{2,1,0:T(8,128)(2,1)}, bf16[24,64,256]{2,1,0:T(8,128)(2,1)}) custom-call(s32[24]{0:T(128)} %select_reduce_fusion.which, bf16[64,128,256]{2,1,0:T(8,128)(2,1)} %all-to-all-done.1.slots), custom_call_target="tpu_custom_call" | custom-call | bytes 4194304 | tf_op jit(solution)/shard_map/pallas_call | solution.py:240
  (14 shorter events, 0.2 us)
Async XLA Ops:
  4.8 12.1 %copy-start = (bf16[384,256]{1,0:T(8,128)(2,1)S(1)}, bf16[384,256]{1,0:T(8,128)(2,1)}, u32[]{:S(2)}) copy-start(bf16[384,256]{1,0:T(8,128)(2,1)} %param.6) | copy-start | bytes 589828
  4.8 12.1 %copy-start.1 = (bf16[384,256]{1,0:T(8,128)(2,1)S(1)}, bf16[384,256]{1,0:T(8,128)(2,1)}, u32[]{:S(2)}) copy-start(bf16[384,256]{1,0:T(8,128)(2,1)} %param.9) | copy-start | bytes 589828
  4.9 14.8 %copy-start.2 = (s32[6,4]{0,1:T(4,128)S(1)}, s32[6,4]{0,1:T(4,128)}, u32[]{:S(2)}) copy-start(s32[6,4]{0,1:T(4,128)} %param.10) | copy-start | bytes 292
  4.9 106.7 %all-to-all-start = ((bf16[64,128,256]{2,1,0:T(8,128)(2,1)}), bf16[64,128,256]{2,1,0:T(8,128)(2,1)}, u32[]{:S(2)}, u32[]{:S(2)}) async-start(bf16[64,128,256]{2,1,0:T(8,128)(2,1)} %shard_map.93), calls=%async_computation | async-start | bytes 8388608 | tf_op jit(solution)/shard_map/all_to_all | solution.py:182
  17.0 14.0 %collective-permute-start = (bf16[2,64,256]{2,1,0:T(8,128)(2,1)S(1)}, bf16[2,64,256]{2,1,0:T(8,128)(2,1)S(1)}, u32[]{:S(2)}, u32[]{:S(2)}) collective-permute-start(bf16[2,64,256]{2,1,0:T(8,128)(2,1)S(1)} %pad_maximum_fusion.4), channel_id=1, source_target_pairs={{8,0},{16,8},{24,16},{32,24},{40,32},{48,40},{56,48},{64,56},{72,6... | collective-permute-start | bytes 196616 | tf_op jit(solution)/shard_map/ppermute | solution.py:178
  119.0 104.0 %all-to-all-start.1 = ((bf16[64,128,256]{2,1,0:T(8,128)(2,1)}), bf16[64,128,256]{2,1,0:T(8,128)(2,1)}, u32[]{:S(2)}, u32[]{:S(2)}) async-start(bf16[64,128,256]{2,1,0:T(8,128)(2,1)} %get-tuple-element.15), calls=%async_computation.1 | async-start | bytes 8388608 | tf_op jit(solution)/shard_map/all_to_all | solution.py:182
  127.3 9.3 %copy-start.3 = (s32[1,64,1]{1,2,0:T(1,128)S(1)}, s32[1,64,1]{1,2,0:T(1,128)}, u32[]{:S(2)}) copy-start(s32[1,64,1]{1,2,0:T(1,128)} %param.11) | copy-start | bytes 772
  133.1 6.1 %collective-permute-start.1 = (bf16[2,64,256]{2,1,0:T(8,128)(2,1)S(1)}, bf16[2,64,256]{2,1,0:T(8,128)(2,1)S(1)}, u32[]{:S(2)}, u32[]{:S(2)}) collective-permute-start(bf16[2,64,256]{2,1,0:T(8,128)(2,1)S(1)} %pad_maximum_fusion.5), channel_id=1, source_target_pairs={{0,8},{8,16},{16,24},{24,32},{32,40},{40,48},{48,56},{56,64},{64,7... | collective-permute-start | bytes 196616 | tf_op jit(solution)/shard_map/ppermute | solution.py:178

commit v4 on v3

v4 whole, which is shorter than its diff:
```python
import jax
import jax.numpy as jnp
from jax import lax
from jax.experimental import pallas as pl
from jax.experimental.pallas import tpu as pltpu
from jax.sharding import PartitionSpec as P

HEAD_DIM = 128
GROUP = 64
PAIR = 2 * GROUP
MIB = 1024 * 1024
SCALE = HEAD_DIM ** (-0.5)
SIDE = 3

VM = pl.BlockSpec(memory_space=pltpu.VMEM)
SM = pl.BlockSpec(memory_space=pltpu.SMEM)
HB = pl.BlockSpec(memory_space=pltpu.HBM)


def call(kernel, in_specs, out_specs, out_shape, scratch=(), flops=0, moved=0, aliases=None, vmem=12):
    return pl.pallas_call(
        kernel,
        out_shape=out_shape,
        in_specs=in_specs,
        out_specs=out_specs,
        scratch_shapes=list(scratch),
        input_output_aliases=aliases or {},
        compiler_params=pltpu.CompilerParams(vmem_limit_bytes=vmem * MIB),
        cost_estimate=pl.CostEstimate(flops=flops, bytes_accessed=moved, transcendentals=0),
    )


def blank_kernel(slots, zeros, sem):
    zeros[...] = jnp.zeros(zeros.shape, zeros.dtype)
    many = zeros.shape[0]
    for first in range(0, slots.shape[0], many):
        pltpu.make_async_copy(zeros, slots.at[pl.ds(first, many)], sem).start()
    pltpu.make_async_copy(slots, slots, sem).wait()


def pack_kernel(table, keys, values, slots, staged, zeros, in_sems, out_sem):
    parts = in_sems.shape[0]
    some = keys.shape[0] // parts
    loads = []
    for part in range(parts):
        own = pl.ds(part * some, some)
        loads.append(pltpu.make_async_copy(keys.at[own], staged.at[own, pl.ds(0, GROUP)], in_sems.at[part, 0]))
        loads.append(pltpu.make_async_copy(values.at[own], staged.at[own, pl.ds(GROUP, GROUP)], in_sems.at[part, 1]))
    for load in loads:
        load.start()
    zeros[...] = jnp.zeros(zeros.shape, zeros.dtype)
    for slot in range(slots.shape[0]):

        @pl.when(table[slot] < 0)
        def _():
            pltpu.make_async_copy(zeros, slots.at[slot], out_sem).start()

    for load in loads:
        load.wait()
    for slot in range(slots.shape[0]):
        unit = table[slot]

        @pl.when(unit >= 0)
        def _():
            pltpu.make_async_copy(staged.at[unit], slots.at[slot], out_sem).start()

    pltpu.make_async_copy(slots, slots, out_sem).wait()


def unpack_kernel(which, slots, keys, values, staged, zeros, in_sems, key_sem, value_sem):
    zeros[...] = jnp.zeros(zeros.shape, zeros.dtype)
    parts = in_sems.shape[0]
    some = keys.shape[0] // parts
    for unit in range(keys.shape[0]):
        slot = which[unit]

        @pl.when(slot >= 0)
        def _():
            pltpu.make_async_copy(slots.at[slot], staged.at[unit], in_sems.at[unit // some]).start()

        @pl.when(slot < 0)
        def _():
            pltpu.make_async_copy(zeros, staged.at[unit], in_sems.at[unit // some]).start()

    for part in range(parts):
        own = pl.ds(part * some, some)
        pltpu.make_async_copy(staged.at[own], staged.at[own], in_sems.at[part]).wait()
        pltpu.make_async_copy(staged.at[own, pl.ds(0, GROUP)], keys.at[own], key_sem).start()
        pltpu.make_async_copy(staged.at[own, pl.ds(GROUP, GROUP)], values.at[own], value_sem).start()
    pltpu.make_async_copy(keys, keys, key_sem).wait()
    pltpu.make_async_copy(values, values, value_sem).wait()


def dot(a, b, contract):
    return lax.dot_general(a, b, ((contract[:1], contract[1:]), ((), ())), preferred_element_type=jnp.float32)


def by_head(rows):
    blank = jnp.zeros((rows.shape[0], HEAD_DIM), rows.dtype)
    heads = rows.shape[1] // HEAD_DIM
    return jnp.concatenate(
        [
            jnp.concatenate(
                [rows[:, h * HEAD_DIM : (h + 1) * HEAD_DIM] if h == at else blank for h in range(heads)], axis=1
            )
            for at in range(heads)
        ],
        axis=0,
    )


def gather(source, slots, blocks, sems):
    groups, per_group = blocks.shape[:2]
    for group in range(groups):
        for j in range(per_group):
            slot = source[group * per_group + j]
            pltpu.make_async_copy(slots.at[slot], blocks.at[group, j], sems.at[group]).start()


def half(blocks, group, part):
    per_group, _, cols = blocks.shape[1:]
    return blocks[group, :, part * GROUP : (part + 1) * GROUP].reshape(per_group * GROUP, cols)


def block_kernel(
    source, queries, grads, slots, blank, send, probs, scores_grad, blocks, block_grads, in_sems, out_sem
):
    groups, per_group, _, cols = blocks.shape
    low = jnp.bfloat16
    gather(source, slots, blocks, in_sems)
    for first in range(0, groups, SIDE):
        side = range(first, min(first + SIDE, groups))
        query = [by_head(queries[g * GROUP : (g + 1) * GROUP]) for g in side]
        grad = [by_head(grads[g * GROUP : (g + 1) * GROUP]) for g in side]
        for g in side:
            pltpu.make_async_copy(blocks.at[g], blocks.at[g], in_sems.at[g]).wait()
        scores = [dot(half(blocks, g, 0), q, (1, 1)) * SCALE for g, q in zip(side, query)]
        grad_probs = [dot(half(blocks, g, 1), d, (1, 1)) for g, d in zip(side, grad)]
        powers = [jnp.exp(s - jnp.max(s, axis=0, keepdims=True)) for s in scores]
        chances = [p * (1.0 / jnp.sum(p, axis=0, keepdims=True)) for p in powers]
        chances_low = [c.astype(low) for c in chances]
        row_dot = [jnp.sum(c * g, axis=0, keepdims=True) for c, g in zip(chances, grad_probs)]
        grad_low = [(c * (g - r) * SCALE).astype(low) for c, g, r in zip(chances, grad_probs, row_dot)]
        value_part = [dot(c, d, (1, 0)).astype(low) for c, d in zip(chances_low, grad)]
        key_part = [dot(g, q, (1, 0)).astype(low) for g, q in zip(grad_low, query)]
        for at, g in enumerate(side):
            probs[g] = chances_low[at]
            scores_grad[g] = grad_low[at]
            block_grads[g, :, :GROUP] = key_part[at].reshape(per_group, GROUP, cols)
            block_grads[g, :, GROUP:] = value_part[at].reshape(per_group, GROUP, cols)
        for g in side:
            for j in range(per_group):
                slot = source[g * per_group + j]
                pltpu.make_async_copy(block_grads.at[g, j], send.at[slot], out_sem).start()
    pltpu.make_async_copy(block_grads, block_grads, out_sem).wait()


def token_kernel(source, probs, scores_grad, slots, attended, query_grad, blocks, in_sems):
    gather(source, slots, blocks, in_sems)
    for group in range(blocks.shape[0]):
        pltpu.make_async_copy(blocks.at[group], blocks.at[group], in_sems.at[group]).wait()
        rows = slice(group * GROUP, (group + 1) * GROUP)
        mixed = dot(probs[group], half(blocks, group, 1), (0, 0)).astype(jnp.bfloat16)
        query_part = dot(scores_grad[group], half(blocks, group, 0), (0, 0)).astype(jnp.bfloat16)
        for head in range(attended.shape[1] // HEAD_DIM):
            own = slice(head * GROUP, (head + 1) * GROUP)
            column = slice(head * HEAD_DIM, (head + 1) * HEAD_DIM)
            attended[rows, column] = mixed[own, column]
            query_grad[rows, column] = query_part[own, column]


def shift(value, axis, steps):
    count = lax.axis_size(axis)
    first, last = max(0, -steps), min(count, count - steps)
    return lax.ppermute(value, axis, [(at, at + steps) for at in range(first, last)])


def exchange(slots):
    return lax.all_to_all(slots, "seq", split_axis=0, concat_axis=0, tiled=True)


def local(queries, neighbor_keys, neighbor_values, out_grad, neighbor_source, send_unit):
    tok_rows, cols = queries.shape
    groups, per_group = neighbor_source.shape
    units = neighbor_keys.shape[0] // GROUP
    slots = send_unit.shape[1] * send_unit.shape[2]
    heads, keys = cols // HEAD_DIM, per_group * GROUP
    low = jnp.bfloat16
    table = send_unit.reshape(slots)
    source = neighbor_source.reshape(units)
    slot_shape = jax.ShapeDtypeStruct((slots, PAIR, cols), low)
    unit_shape = jax.ShapeDtypeStruct((units, GROUP, cols), low)
    tok_shape = jax.ShapeDtypeStruct((tok_rows, cols), low)
    prob_shape = jax.ShapeDtypeStruct((groups, keys, heads * GROUP), low)
    slot_bytes = slots * PAIR * cols * 2
    matmul = 2 * groups * keys * heads * GROUP * cols
    sem = pltpu.SemaphoreType.DMA
    blocks = pltpu.VMEM((groups, per_group, PAIR, cols), low)
    staged = pltpu.VMEM((units, PAIR, cols), low)
    group_sems = pltpu.SemaphoreType.DMA((groups,))

    received = exchange(
        call(
            pack_kernel, [SM, HB, HB], HB, pltpu.HBM(slot_shape.shape, low),
            scratch=[
                staged, pltpu.VMEM((PAIR, cols), low),
                pltpu.SemaphoreType.DMA((2, 2)), sem,
            ],
            moved=2 * slot_bytes, vmem=58,
        )(table, neighbor_keys.reshape(unit_shape.shape), neighbor_values.reshape(unit_shape.shape))
    )
    blank = call(
        blank_kernel, [], HB, pltpu.HBM(slot_shape.shape, low),
        scratch=[pltpu.VMEM((8, PAIR, cols), low), sem], moved=slot_bytes,
    )()

    edge = GROUP - 1
    ahead = shift(jnp.stack([queries[:GROUP], out_grad[:GROUP]]), "seq", -1)
    group_queries = jnp.concatenate([queries[edge:], ahead[0, :edge]], axis=0)
    group_grads = jnp.concatenate([out_grad[edge:], ahead[1, :edge]], axis=0)
    fills = table[None, :] == jnp.arange(units, dtype=jnp.int32)[:, None]
    which = jnp.max(jnp.where(fills, jnp.arange(slots, dtype=jnp.int32)[None, :], -1), axis=1)

    send, probs, scores_grad = call(
        block_kernel, [SM, VM, VM, HB, HB], (HB, VM, VM), (pltpu.HBM(slot_shape.shape, low), prob_shape, prob_shape),
        scratch=[blocks, blocks, group_sems, sem],
        flops=4 * matmul, moved=slot_bytes, aliases={4: 0}, vmem=58,
    )(source, group_queries, group_grads, received, blank)
    returned = exchange(send)

    mixed, query_part = call(
        token_kernel, [SM, VM, VM, HB], (VM, VM), (tok_shape, tok_shape),
        scratch=[blocks, group_sems], flops=2 * matmul, moved=slot_bytes,
    )(source, probs, scores_grad, received)
    behind = shift(jnp.stack([mixed[-GROUP:], query_part[-GROUP:]]), "seq", 1)
    attended = jnp.concatenate([behind[0, 1:], mixed[: tok_rows - edge]], axis=0)
    query_grad = jnp.concatenate([behind[1, 1:], query_part[: tok_rows - edge]], axis=0)

    unit_out = pltpu.HBM(unit_shape.shape, low)
    key_grad, value_grad = call(
        unpack_kernel, [SM, HB], (HB, HB), (unit_out, unit_out),
        scratch=[staged, pltpu.VMEM((PAIR, cols), low), pltpu.SemaphoreType.DMA((4,)), sem, sem],
        moved=slot_bytes, vmem=58,
    )(which, returned)
    flat = (units * GROUP, cols)
    return (attended, query_grad, key_grad.reshape(flat), value_grad.reshape(flat))


def solution(mesh):
    return jax.shard_map(
        local,
        mesh=mesh,
        in_specs=(
            P("seq", "mp"),
            P("seq", "mp"),
            P("seq", "mp"),
            P("seq", "mp"),
            P("seq", None),
            P("seq", None, None),
        ),
        out_specs=(P("seq", "mp"), P("seq", "mp"), P("seq", "mp"), P("seq", "mp")),
        check_vma=False,
    )
```

time: 227 us -> 225 us (level)
  local copies, waits for them, and re-layouts: 4.22 us -> 0.94 us
  waiting for transfers between devices: 172 us -> 175 us
    pallas_call x3 -> x4, Pallas kernels: 14.6 us -> 14.5 us  [the longest x1 5.36 us: local(): call(block_kernel, [SM, VM, VM, HB, HB], (HB, VM, VM), (pltpu.HBM(slot_sh...]
  transfers between devices with their start and end apart: 4 -> 4, of which waited for: 3 -> 4; matrix products, arithmetic and copies ran while one was open for 3% -> 2% of each run, Pallas kernels for 2% -> 2%
where the time goes in v4:
time: 225 us; the launch traced here: 224 us
  waiting for transfers between devices  175 us (78%)
  starting transfers between devices  26.6 us (12%)
  Pallas kernels  17.4 us (8%)
  other arithmetic  3.49 us (2%)
    all_to_all x2, waiting for transfers between devices, exchange(): return lax.all_to_all(slots, 'seq', split_axis=0, concat_axis=0, tiled=True)  163 us
    all_to_all x2, starting transfers between devices, exchange(): return lax.all_to_all(slots, 'seq', split_axis=0, concat_axis=0, tiled=True)  20.5 us
    ppermute x2, waiting for transfers between devices, shift(): lax.ppermute(value, axis, [(at, at + steps) for at in range(first, last)])  12 us
    ppermute x2, starting transfers between devices, shift(): lax.ppermute(value, axis, [(at, at + steps) for at in range(first, last)])  6.09 us
    pallas_call x1, Pallas kernels, local(): call(block_kernel, [SM, VM, VM, HB, HB], (HB, VM, VM), (pltpu.HBM(slot_sh...  5.36 us
  transfers between devices with their start and end apart: 4, of which 4 were waited for; matrix products, arithmetic and copies ran while one was open for 2% of the time, Pallas kernels for 2%

profile of v4, /device:TPU:1, one launch (start us, length us, event | category | flops | bytes accessed | tf_op | source)
XLA Modules:
  0.0 224.0 jit_solution(14084307482932794118)
XLA Ops:
  0.6 4.2 %shard_map.93 = bf16[64,128,256]{2,1,0:T(8,128)(2,1)} custom-call(s32[64]{0:T(128)} %bitcast.23, bf16[24,64,256]{2,1,0:T(8,128)(2,1)} %bitcast.21, bf16[24,64,256]{2,1,0:T(8,128)(2,1)} %bitcast.22), custom_call_target="tpu_custom_call" | custom-call | bytes 8388608 | tf_op jit(solution)/shard_map/pallas_call | solution.py:203
  4.8 0.0 copy-start.3
  4.8 0.0 copy-start.4
  4.9 12.0 %all-to-all-start = ((bf16[64,128,256]{2,1,0:T(8,128)(2,1)}), bf16[64,128,256]{2,1,0:T(8,128)(2,1)}, u32[]{:S(2)}, u32[]{:S(2)}) async-start(bf16[64,128,256]{2,1,0:T(8,128)(2,1)} %shard_map.93), calls=%async_computation | async-start | bytes 8388608 | tf_op jit(solution)/shard_map/all_to_all | solution.py:179
  17.0 2.5 %collective-permute-start = (bf16[2,64,256]{2,1,0:T(8,128)(2,1)S(1)}, bf16[2,64,256]{2,1,0:T(8,128)(2,1)S(1)}, u32[]{:S(2)}, u32[]{:S(2)}) collective-permute-start(bf16[2,64,256]{2,1,0:T(8,128)(2,1)S(1)} %pad_maximum_fusion.4), channel_id=1, source_target_pairs={{8,0},{16,8},{24,16},{32,24},{40,32},{48,40},{56,48},{64,56},{72,6... | collective-permute-start | bytes 196616 | tf_op jit(solution)/shard_map/ppermute | solution.py:175
  19.6 2.0 shard_map.94.blank
  21.6 0.1 copy.13
  21.7 0.7 reshape.27.source
  22.4 8.6 %collective-permute-done = bf16[2,64,256]{2,1,0:T(8,128)(2,1)S(1)} collective-permute-done((bf16[2,64,256]{2,1,0:T(8,128)(2,1)S(1)}, bf16[2,64,256]{2,1,0:T(8,128)(2,1)S(1)}, u32[]{:S(2)}, u32[]{:S(2)}) %collective-permute-start) | collective-permute-done | bytes 65568 | tf_op jit(solution)/shard_map/ppermute | solution.py:175
  31.0 0.7 pad_maximum_fusion.queries
  31.7 0.7 pad_maximum_fusion.1.grads
  32.4 79.2 %all-to-all-done.slots = bf16[64,128,256]{2,1,0:T(8,128)(2,1)} async-done(((bf16[64,128,256]{2,1,0:T(8,128)(2,1)}), bf16[64,128,256]{2,1,0:T(8,128)(2,1)}, u32[]{:S(2)}, u32[]{:S(2)}) %all-to-all-start) | async-done | bytes 4194336 | tf_op jit(solution)/shard_map/all_to_all | solution.py:179
  111.6 5.4 %shard_map.95 = (bf16[64,128,256]{2,1,0:T(8,128)(2,1)}, bf16[6,256,128]{2,1,0:T(8,128)(2,1)}, bf16[6,256,128]{2,1,0:T(8,128)(2,1)}) custom-call(s32[24]{0:T(128)} %reshape.27.source, bf16[384,256]{1,0:T(8,128)(2,1)} %pad_maximum_fusion.queries, bf16[384,256]{1,0:T(8,128)(2,1)} %pad_maximum_fusion.1.grads, ...), custom_call_target="tpu_custom_call", output_to_operand_aliasing={{0}: (4, {})} | custom-call | flops 402653184 | bytes 4194304 | tf_op jit(solution)/shard_map/pallas_call | solution.py:224
  116.9 0.0 copy-start.1
  117.0 8.5 %all-to-all-start.1 = ((bf16[64,128,256]{2,1,0:T(8,128)(2,1)}), bf16[64,128,256]{2,1,0:T(8,128)(2,1)}, u32[]{:S(2)}, u32[]{:S(2)}) async-start(bf16[64,128,256]{2,1,0:T(8,128)(2,1)} %get-tuple-element.15), calls=%async_computation.1 | async-start | bytes 8388608 | tf_op jit(solution)/shard_map/all_to_all | solution.py:179
  125.4 0.0 copy-start.6
  125.5 2.9 %shard_map.96 = (bf16[384,256]{1,0:T(8,128)(2,1)S(1)}, bf16[384,256]{1,0:T(8,128)(2,1)S(1)}) custom-call(s32[24]{0:T(128)S(1)} %copy-done.2, bf16[6,256,128]{2,1,0:T(8,128)(2,1)S(1)} %copy-done, bf16[6,256,128]{2,1,0:T(8,128)(2,1)S(1)} %copy-done.1, bf16[64,128,256]{2,1,0:T(8,128)(2,1)} %all-to-all-done.slots), custom_call_target="tpu_custom_call" | custom-call | flops 201326592 | bytes 4194304 | tf_op jit(solution)/shard_map/pallas_call | solution.py:231
  128.4 3.5 %collective-permute-start.1 = (bf16[2,64,256]{2,1,0:T(8,128)(2,1)S(1)}, bf16[2,64,256]{2,1,0:T(8,128)(2,1)S(1)}, u32[]{:S(2)}, u32[]{:S(2)}) collective-permute-start(bf16[2,64,256]{2,1,0:T(8,128)(2,1)S(1)} %pad_maximum_fusion.5), channel_id=1, source_target_pairs={{0,8},{8,16},{16,24},{24,32},{32,40},{40,48},{48,56},{56,64},{64,7... | collective-permute-start | bytes 196616 | tf_op jit(solution)/shard_map/ppermute | solution.py:175
  132.0 0.6 select_reduce_fusion.which
  132.7 3.4 %collective-permute-done.1 = bf16[2,64,256]{2,1,0:T(8,128)(2,1)S(1)} collective-permute-done((bf16[2,64,256]{2,1,0:T(8,128)(2,1)S(1)}, bf16[2,64,256]{2,1,0:T(8,128)(2,1)S(1)}, u32[]{:S(2)}, u32[]{:S(2)}) %collective-permute-start.1) | collective-permute-done | bytes 65568 | tf_op jit(solution)/shard_map/ppermute | solution.py:175
  136.1 0.7 pad_maximum_fusion.3
  136.8 0.7 pad_maximum_fusion.2
  137.5 83.6 %all-to-all-done.1.slots = bf16[64,128,256]{2,1,0:T(8,128)(2,1)} async-done(((bf16[64,128,256]{2,1,0:T(8,128)(2,1)}), bf16[64,128,256]{2,1,0:T(8,128)(2,1)}, u32[]{:S(2)}, u32[]{:S(2)}) %all-to-all-start.1) | async-done | bytes 4194336 | tf_op jit(solution)/shard_map/all_to_all | solution.py:179
  221.2 2.9 %shard_map.97 = (bf16[24,64,256]{2,1,0:T(8,128)(2,1)}, bf16[24,64,256]{2,1,0:T(8,128)(2,1)}) custom-call(s32[24]{0:T(128)} %select_reduce_fusion.which, bf16[64,128,256]{2,1,0:T(8,128)(2,1)} %all-to-all-done.1.slots), custom_call_target="tpu_custom_call" | custom-call | bytes 4194304 | tf_op jit(solution)/shard_map/pallas_call | solution.py:240
  (21 shorter events, 0.2 us)
Async XLA Ops:
  4.8 12.1 %copy-start.3 = (bf16[384,256]{1,0:T(8,128)(2,1)S(1)}, bf16[384,256]{1,0:T(8,128)(2,1)}, u32[]{:S(2)}) copy-start(bf16[384,256]{1,0:T(8,128)(2,1)} %param.6) | copy-start | bytes 589828
  4.8 12.1 %copy-start.4 = (bf16[384,256]{1,0:T(8,128)(2,1)S(1)}, bf16[384,256]{1,0:T(8,128)(2,1)}, u32[]{:S(2)}) copy-start(bf16[384,256]{1,0:T(8,128)(2,1)} %param.9) | copy-start | bytes 589828
  4.9 106.7 %all-to-all-start = ((bf16[64,128,256]{2,1,0:T(8,128)(2,1)}), bf16[64,128,256]{2,1,0:T(8,128)(2,1)}, u32[]{:S(2)}, u32[]{:S(2)}) async-start(bf16[64,128,256]{2,1,0:T(8,128)(2,1)} %shard_map.93), calls=%async_computation | async-start | bytes 8388608 | tf_op jit(solution)/shard_map/all_to_all | solution.py:179
  16.9 4.7 %copy-start.5 = (s32[6,4]{0,1:T(4,128)S(1)}, s32[6,4]{0,1:T(4,128)}, u32[]{:S(2)}) copy-start(s32[6,4]{0,1:T(4,128)} %param.10) | copy-start | bytes 292
  17.0 14.0 %collective-permute-start = (bf16[2,64,256]{2,1,0:T(8,128)(2,1)S(1)}, bf16[2,64,256]{2,1,0:T(8,128)(2,1)S(1)}, u32[]{:S(2)}, u32[]{:S(2)}) collective-permute-start(bf16[2,64,256]{2,1,0:T(8,128)(2,1)S(1)} %pad_maximum_fusion.4), channel_id=1, source_target_pairs={{8,0},{16,8},{24,16},{32,24},{40,32},{48,40},{56,48},{64,56},{72,6... | collective-permute-start | bytes 196616 | tf_op jit(solution)/shard_map/ppermute | solution.py:175
  116.9 8.5 %copy-start = (bf16[6,256,128]{2,1,0:T(8,128)(2,1)S(1)}, bf16[6,256,128]{2,1,0:T(8,128)(2,1)}, u32[]{:S(2)}) copy-start(bf16[6,256,128]{2,1,0:T(8,128)(2,1)} %get-tuple-element.11.probs) | copy-start | bytes 1179652
  116.9 8.5 %copy-start.1 = (bf16[6,256,128]{2,1,0:T(8,128)(2,1)S(1)}, bf16[6,256,128]{2,1,0:T(8,128)(2,1)}, u32[]{:S(2)}) copy-start(bf16[6,256,128]{2,1,0:T(8,128)(2,1)} %get-tuple-element.12.scores_grad) | copy-start | bytes 1179652
  116.9 8.5 %copy-start.2 = (s32[24]{0:T(128)S(1)}, s32[24]{0:T(128)}, u32[]{:S(2)}) copy-start(s32[24]{0:T(128)} %reshape.27.source) | copy-start | bytes 292
  117.0 104.2 %all-to-all-start.1 = ((bf16[64,128,256]{2,1,0:T(8,128)(2,1)}), bf16[64,128,256]{2,1,0:T(8,128)(2,1)}, u32[]{:S(2)}, u32[]{:S(2)}) async-start(bf16[64,128,256]{2,1,0:T(8,128)(2,1)} %get-tuple-element.15), calls=%async_computation.1 | async-start | bytes 8388608 | tf_op jit(solution)/shard_map/all_to_all | solution.py:179
  125.4 6.5 %copy-start.6 = (s32[1,64,1]{1,2,0:T(1,128)S(1)}, s32[1,64,1]{1,2,0:T(1,128)}, u32[]{:S(2)}) copy-start(s32[1,64,1]{1,2,0:T(1,128)} %param.11) | copy-start | bytes 772
  128.4 7.6 %collective-permute-start.1 = (bf16[2,64,256]{2,1,0:T(8,128)(2,1)S(1)}, bf16[2,64,256]{2,1,0:T(8,128)(2,1)S(1)}, u32[]{:S(2)}, u32[]{:S(2)}) collective-permute-start(bf16[2,64,256]{2,1,0:T(8,128)(2,1)S(1)} %pad_maximum_fusion.5), channel_id=1, source_target_pairs={{0,8},{8,16},{16,24},{24,32},{32,40},{40,48},{48,56},{56,64},{64,7... | collective-permute-start | bytes 196616 | tf_op jit(solution)/shard_map/ppermute | solution.py:175

commit v5 on v4

--- a/solution.py
+++ b/solution.py
@@ -224,7 +224,7 @@
     send, probs, scores_grad = call(
         block_kernel, [SM, VM, VM, HB, HB], (HB, VM, VM), (pltpu.HBM(slot_shape.shape, low), prob_shape, prob_shape),
         scratch=[blocks, blocks, group_sems, sem],
-        flops=4 * matmul, moved=slot_bytes, aliases={4: 0}, vmem=58,
+        flops=4 * matmul, moved=slot_bytes, aliases={4: 0}, vmem=16,
     )(source, group_queries, group_grads, received, blank)
     returned = exchange(send)
 

time: 225 us -> 222 us (0.987)
  transfers between devices with their start and end apart: 4 -> 4, of which waited for: 4 -> 4; matrix products, arithmetic and copies ran while one was open for 2% -> 1% of each run, Pallas kernels for 2% -> 2%
where the time goes in v5:
time: 222 us; the launch traced here: 221 us
  waiting for transfers between devices  177 us (80%)
  starting transfers between devices  25.3 us (11%)
  Pallas kernels  16 us (7%)
    all_to_all x2, waiting for transfers between devices, exchange(): return lax.all_to_all(slots, 'seq', split_axis=0, concat_axis=0, tiled=True)  164 us
    all_to_all x2, starting transfers between devices, exchange(): return lax.all_to_all(slots, 'seq', split_axis=0, concat_axis=0, tiled=True)  19.2 us
    ppermute x2, waiting for transfers between devices, shift(): lax.ppermute(value, axis, [(at, at + steps) for at in range(first, last)])  12.4 us
    ppermute x2, starting transfers between devices, shift(): lax.ppermute(value, axis, [(at, at + steps) for at in range(first, last)])  6.09 us
  transfers between devices with their start and end apart: 4, of which 4 were waited for; matrix products, arithmetic and copies ran while one was open for 1% of the time, Pallas kernels for 2%

profile of v5, /device:TPU:1, one launch (start us, length us, event | category | flops | bytes accessed | tf_op | source)
XLA Modules:
  0.0 221.5 jit_solution(6441478004224603326)
XLA Ops:
  0.6 4.2 %shard_map.93 = bf16[64,128,256]{2,1,0:T(8,128)(2,1)} custom-call(s32[64]{0:T(128)} %bitcast.23, bf16[24,64,256]{2,1,0:T(8,128)(2,1)} %bitcast.21, bf16[24,64,256]{2,1,0:T(8,128)(2,1)} %bitcast.22), custom_call_target="tpu_custom_call" | custom-call | bytes 8388608 | tf_op jit(solution)/shard_map/pallas_call | solution.py:203
  4.8 0.0 copy-start
  4.8 0.0 copy-start.1
  4.8 12.0 %all-to-all-start = ((bf16[64,128,256]{2,1,0:T(8,128)(2,1)}), bf16[64,128,256]{2,1,0:T(8,128)(2,1)}, u32[]{:S(2)}, u32[]{:S(2)}) async-start(bf16[64,128,256]{2,1,0:T(8,128)(2,1)} %shard_map.93), calls=%async_computation | async-start | bytes 8388608 | tf_op jit(solution)/shard_map/all_to_all | solution.py:179
  16.9 0.0 copy-done
  16.9 0.0 copy-start.2
  16.9 2.5 %collective-permute-start = (bf16[2,64,256]{2,1,0:T(8,128)(2,1)S(1)}, bf16[2,64,256]{2,1,0:T(8,128)(2,1)S(1)}, u32[]{:S(2)}, u32[]{:S(2)}) collective-permute-start(bf16[2,64,256]{2,1,0:T(8,128)(2,1)S(1)} %pad_maximum_fusion.4), channel_id=1, source_target_pairs={{8,0},{16,8},{24,16},{32,24},{40,32},{48,40},{56,48},{64,56},{72,6... | collective-permute-start | bytes 196616 | tf_op jit(solution)/shard_map/ppermute | solution.py:175
  19.6 2.0 shard_map.94.blank
  21.6 0.1 copy.13
  21.7 0.1 reshape.27.source
  21.8 9.2 %collective-permute-done = bf16[2,64,256]{2,1,0:T(8,128)(2,1)S(1)} collective-permute-done((bf16[2,64,256]{2,1,0:T(8,128)(2,1)S(1)}, bf16[2,64,256]{2,1,0:T(8,128)(2,1)S(1)}, u32[]{:S(2)}, u32[]{:S(2)}) %collective-permute-start) | collective-permute-done | bytes 65568 | tf_op jit(solution)/shard_map/ppermute | solution.py:175
  31.0 80.5 %all-to-all-done.slots = bf16[64,128,256]{2,1,0:T(8,128)(2,1)} async-done(((bf16[64,128,256]{2,1,0:T(8,128)(2,1)}), bf16[64,128,256]{2,1,0:T(8,128)(2,1)}, u32[]{:S(2)}, u32[]{:S(2)}) %all-to-all-start) | async-done | bytes 4194336 | tf_op jit(solution)/shard_map/all_to_all | solution.py:179
  111.5 4.0 %shard_map.95 = (bf16[64,128,256]{2,1,0:T(8,128)(2,1)}, bf16[6,256,128]{2,1,0:T(8,128)(2,1)S(1)}, bf16[6,256,128]{2,1,0:T(8,128)(2,1)S(1)}) custom-call(s32[24]{0:T(128)S(1)} %reshape.27.source, bf16[384,256]{1,0:T(8,128)(2,1)S(1)} %pad_maximum_fusion.queries, bf16[384,256]{1,0:T(8,128)(2,1)S(1)} %pad_maximum_fusion.1.grads, ...), custom_call_target="tpu_custom_call", output_to_operand_aliasing={{0}: (4, {})} | custom-call | flops 402653184 | bytes 4194304 | tf_op jit(solution)/shard_map/pallas_call | solution.py:224
  115.5 7.2 %all-to-all-start.1 = ((bf16[64,128,256]{2,1,0:T(8,128)(2,1)}), bf16[64,128,256]{2,1,0:T(8,128)(2,1)}, u32[]{:S(2)}, u32[]{:S(2)}) async-start(bf16[64,128,256]{2,1,0:T(8,128)(2,1)} %get-tuple-element.15), calls=%async_computation.1 | async-start | bytes 8388608 | tf_op jit(solution)/shard_map/all_to_all | solution.py:179
  122.8 0.0 copy-start.3
  122.8 2.9 %shard_map.96 = (bf16[384,256]{1,0:T(8,128)(2,1)S(1)}, bf16[384,256]{1,0:T(8,128)(2,1)S(1)}) custom-call(s32[24]{0:T(128)S(1)} %reshape.27.source, bf16[6,256,128]{2,1,0:T(8,128)(2,1)S(1)} %get-tuple-element.11.probs, bf16[6,256,128]{2,1,0:T(8,128)(2,1)S(1)} %get-tuple-element.12.scores_grad, bf16[64,128,256]{2,1,0:T(8,128)(2,1)} %all-to-all-done.slots), custom_call_target="tpu_custom_call" | custom-call | flops 201326592 | bytes 4194304 | tf_op jit(solution)/shard_map/pallas_call | solution.py:231
  125.7 3.5 %collective-permute-start.1 = (bf16[2,64,256]{2,1,0:T(8,128)(2,1)S(1)}, bf16[2,64,256]{2,1,0:T(8,128)(2,1)S(1)}, u32[]{:S(2)}, u32[]{:S(2)}) collective-permute-start(bf16[2,64,256]{2,1,0:T(8,128)(2,1)S(1)} %pad_maximum_fusion.5), channel_id=1, source_target_pairs={{0,8},{8,16},{16,24},{24,32},{32,40},{40,48},{48,56},{56,64},{64,7... | collective-permute-start | bytes 196616 | tf_op jit(solution)/shard_map/ppermute | solution.py:175
  129.3 0.0 copy-done.3
  129.3 0.6 select_reduce_fusion.which
  130.0 3.2 %collective-permute-done.1 = bf16[2,64,256]{2,1,0:T(8,128)(2,1)S(1)} collective-permute-done((bf16[2,64,256]{2,1,0:T(8,128)(2,1)S(1)}, bf16[2,64,256]{2,1,0:T(8,128)(2,1)S(1)}, u32[]{:S(2)}, u32[]{:S(2)}) %collective-permute-start.1) | collective-permute-done | bytes 65568 | tf_op jit(solution)/shard_map/ppermute | solution.py:175
  133.2 0.7 pad_maximum_fusion.3
  133.9 0.7 pad_maximum_fusion.2
  134.6 84.0 %all-to-all-done.1.slots = bf16[64,128,256]{2,1,0:T(8,128)(2,1)} async-done(((bf16[64,128,256]{2,1,0:T(8,128)(2,1)}), bf16[64,128,256]{2,1,0:T(8,128)(2,1)}, u32[]{:S(2)}, u32[]{:S(2)}) %all-to-all-start.1) | async-done | bytes 4194336 | tf_op jit(solution)/shard_map/all_to_all | solution.py:179
  218.6 2.9 %shard_map.97 = (bf16[24,64,256]{2,1,0:T(8,128)(2,1)}, bf16[24,64,256]{2,1,0:T(8,128)(2,1)}) custom-call(s32[24]{0:T(128)} %select_reduce_fusion.which, bf16[64,128,256]{2,1,0:T(8,128)(2,1)} %all-to-all-done.1.slots), custom_call_target="tpu_custom_call" | custom-call | bytes 4194304 | tf_op jit(solution)/shard_map/pallas_call | solution.py:240
  (15 shorter events, 0.2 us)
Async XLA Ops:
  4.8 12.0 %copy-start = (bf16[384,256]{1,0:T(8,128)(2,1)S(1)}, bf16[384,256]{1,0:T(8,128)(2,1)}, u32[]{:S(2)}) copy-start(bf16[384,256]{1,0:T(8,128)(2,1)} %param.6) | copy-start | bytes 589828
  4.8 12.0 %copy-start.1 = (bf16[384,256]{1,0:T(8,128)(2,1)S(1)}, bf16[384,256]{1,0:T(8,128)(2,1)}, u32[]{:S(2)}) copy-start(bf16[384,256]{1,0:T(8,128)(2,1)} %param.9) | copy-start | bytes 589828
  4.8 106.7 %all-to-all-start = ((bf16[64,128,256]{2,1,0:T(8,128)(2,1)}), bf16[64,128,256]{2,1,0:T(8,128)(2,1)}, u32[]{:S(2)}, u32[]{:S(2)}) async-start(bf16[64,128,256]{2,1,0:T(8,128)(2,1)} %shard_map.93), calls=%async_computation | async-start | bytes 8388608 | tf_op jit(solution)/shard_map/all_to_all | solution.py:179
  16.9 4.7 %copy-start.2 = (s32[6,4]{0,1:T(4,128)S(1)}, s32[6,4]{0,1:T(4,128)}, u32[]{:S(2)}) copy-start(s32[6,4]{0,1:T(4,128)} %param.10) | copy-start | bytes 292
  16.9 14.0 %collective-permute-start = (bf16[2,64,256]{2,1,0:T(8,128)(2,1)S(1)}, bf16[2,64,256]{2,1,0:T(8,128)(2,1)S(1)}, u32[]{:S(2)}, u32[]{:S(2)}) collective-permute-start(bf16[2,64,256]{2,1,0:T(8,128)(2,1)S(1)} %pad_maximum_fusion.4), channel_id=1, source_target_pairs={{8,0},{16,8},{24,16},{32,24},{40,32},{48,40},{56,48},{64,56},{72,6... | collective-permute-start | bytes 196616 | tf_op jit(solution)/shard_map/ppermute | solution.py:175
  115.5 103.1 %all-to-all-start.1 = ((bf16[64,128,256]{2,1,0:T(8,128)(2,1)}), bf16[64,128,256]{2,1,0:T(8,128)(2,1)}, u32[]{:S(2)}, u32[]{:S(2)}) async-start(bf16[64,128,256]{2,1,0:T(8,128)(2,1)} %get-tuple-element.15), calls=%async_computation.1 | async-start | bytes 8388608 | tf_op jit(solution)/shard_map/all_to_all | solution.py:179
  122.8 6.5 %copy-start.3 = (s32[1,64,1]{1,2,0:T(1,128)S(1)}, s32[1,64,1]{1,2,0:T(1,128)}, u32[]{:S(2)}) copy-start(s32[1,64,1]{1,2,0:T(1,128)} %param.11) | copy-start | bytes 772
  125.7 7.4 %collective-permute-start.1 = (bf16[2,64,256]{2,1,0:T(8,128)(2,1)S(1)}, bf16[2,64,256]{2,1,0:T(8,128)(2,1)S(1)}, u32[]{:S(2)}, u32[]{:S(2)}) collective-permute-start(bf16[2,64,256]{2,1,0:T(8,128)(2,1)S(1)} %pad_maximum_fusion.5), channel_id=1, source_target_pairs={{0,8},{8,16},{16,24},{24,32},{32,40},{40,48},{48,56},{56,64},{64,7... | collective-permute-start | bytes 196616 | tf_op jit(solution)/shard_map/ppermute | solution.py:175

commit v6 on v5

--- a/solution.py
+++ b/solution.py
@@ -1,3 +1,5 @@
+import functools
+
 import jax
 import jax.numpy as jnp
 from jax import lax
@@ -11,6 +13,7 @@
 MIB = 1024 * 1024
 SCALE = HEAD_DIM ** (-0.5)
 SIDE = 3
+ROWS = 8
 
 VM = pl.BlockSpec(memory_space=pltpu.VMEM)
 SM = pl.BlockSpec(memory_space=pltpu.SMEM)
@@ -38,7 +41,15 @@
     pltpu.make_async_copy(slots, slots, sem).wait()
 
 
-def pack_kernel(table, keys, values, slots, staged, zeros, in_sems, out_sem):
+def place(slot, count, cap):
+    at, entry = slot // cap, slot % cap
+    row = count // ROWS
+    y, rest = at // row, at % row
+    y = y % (ROWS // 2) * 2 + y // (ROWS // 2)
+    return (y * row + rest) * cap + entry
+
+
+def pack_kernel(count, cap, table, keys, values, slots, staged, zeros, in_sems, out_sem):
     parts = in_sems.shape[0]
     some = keys.shape[0] // parts
     loads = []
@@ -53,7 +64,7 @@
 
         @pl.when(table[slot] < 0)
         def _():
-            pltpu.make_async_copy(zeros, slots.at[slot], out_sem).start()
+            pltpu.make_async_copy(zeros, slots.at[place(slot, count, cap)], out_sem).start()
 
     for load in loads:
         load.wait()
@@ -62,7 +73,7 @@
 
         @pl.when(unit >= 0)
         def _():
-            pltpu.make_async_copy(staged.at[unit], slots.at[slot], out_sem).start()
+            pltpu.make_async_copy(staged.at[unit], slots.at[place(slot, count, cap)], out_sem).start()
 
     pltpu.make_async_copy(slots, slots, out_sem).wait()
 
@@ -176,18 +187,21 @@
 
 
 def exchange(slots):
-    return lax.all_to_all(slots, "seq", split_axis=0, concat_axis=0, tiled=True)
+    count = lax.axis_size("seq")
+    order = sorted(range(count), key=lambda at: place(at, count, 1))
+    return lax.all_to_all(slots, "seq", split_axis=0, concat_axis=0, tiled=True, axis_index_groups=[order])
 
 
 def local(queries, neighbor_keys, neighbor_values, out_grad, neighbor_source, send_unit):
     tok_rows, cols = queries.shape
     groups, per_group = neighbor_source.shape
     units = neighbor_keys.shape[0] // GROUP
-    slots = send_unit.shape[1] * send_unit.shape[2]
+    count, cap = send_unit.shape[1:]
+    slots = count * cap
     heads, keys = cols // HEAD_DIM, per_group * GROUP
     low = jnp.bfloat16
     table = send_unit.reshape(slots)
-    source = neighbor_source.reshape(units)
+    source = place(neighbor_source.reshape(units), count, cap)
     slot_shape = jax.ShapeDtypeStruct((slots, PAIR, cols), low)
     unit_shape = jax.ShapeDtypeStruct((units, GROUP, cols), low)
     tok_shape = jax.ShapeDtypeStruct((tok_rows, cols), low)
@@ -201,7 +215,7 @@
 
     received = exchange(
         call(
-            pack_kernel, [SM, HB, HB], HB, pltpu.HBM(slot_shape.shape, low),
+            functools.partial(pack_kernel, count, cap), [SM, HB, HB], HB, pltpu.HBM(slot_shape.shape, low),
             scratch=[
                 staged, pltpu.VMEM((PAIR, cols), low),
                 pltpu.SemaphoreType.DMA((2, 2)), sem,
@@ -219,7 +233,7 @@
     group_queries = jnp.concatenate([queries[edge:], ahead[0, :edge]], axis=0)
     group_grads = jnp.concatenate([out_grad[edge:], ahead[1, :edge]], axis=0)
     fills = table[None, :] == jnp.arange(units, dtype=jnp.int32)[:, None]
-    which = jnp.max(jnp.where(fills, jnp.arange(slots, dtype=jnp.int32)[None, :], -1), axis=1)
+    which = jnp.max(jnp.where(fills, place(jnp.arange(slots, dtype=jnp.int32), count, cap)[None, :], -1), axis=1)
 
     send, probs, scores_grad = call(
         block_kernel, [SM, VM, VM, HB, HB], (HB, VM, VM), (pltpu.HBM(slot_shape.shape, low), prob_shape, prob_shape),

time: 222 us -> 222 us (level)
  no operation moved by 1% of the time
where the time goes in v6:
time: 222 us; the launch traced here: 221 us
  waiting for transfers between devices  177 us (80%)
  starting transfers between devices  24.5 us (11%)
  Pallas kernels  16 us (7%)
    all_to_all x2, waiting for transfers between devices, exchange(): lax.all_to_all(slots, 'seq', split_axis=0, concat_axis=0, tiled=True, axi...  163 us
    all_to_all x2, starting transfers between devices, exchange(): lax.all_to_all(slots, 'seq', split_axis=0, concat_axis=0, tiled=True, axi...  18.4 us
    ppermute x2, waiting for transfers between devices, shift(): lax.ppermute(value, axis, [(at, at + steps) for at in range(first, last)])  13.7 us
    ppermute x2, starting transfers between devices, shift(): lax.ppermute(value, axis, [(at, at + steps) for at in range(first, last)])  6.09 us
  transfers between devices with their start and end apart: 4, of which 4 were waited for; matrix products, arithmetic and copies ran while one was open for 1% of the time, Pallas kernels for 2%

profile of v6, /device:TPU:1, one launch (start us, length us, event | category | flops | bytes accessed | tf_op | source)
XLA Modules:
  0.0 220.8 jit_solution(17991249959519736676)
XLA Ops:
  0.6 4.2 %shard_map.93 = bf16[64,128,256]{2,1,0:T(8,128)(2,1)} custom-call(s32[64]{0:T(128)} %bitcast.23, bf16[24,64,256]{2,1,0:T(8,128)(2,1)} %bitcast.21, bf16[24,64,256]{2,1,0:T(8,128)(2,1)} %bitcast.22), custom_call_target="tpu_custom_call" | custom-call | bytes 8388608 | tf_op jit(solution)/shard_map/pallas_call | solution.py:217
  4.8 0.0 copy-start
  4.8 0.0 copy-start.1
  4.9 0.0 copy-start.2
  4.9 12.0 %all-to-all-start = ((bf16[64,128,256]{2,1,0:T(8,128)(2,1)}), bf16[64,128,256]{2,1,0:T(8,128)(2,1)}, u32[]{:S(2)}, u32[]{:S(2)}) async-start(bf16[64,128,256]{2,1,0:T(8,128)(2,1)} %shard_map.93), calls=%async_computation | async-start | bytes 8388608 | tf_op jit(solution)/shard_map/all_to_all | solution.py:192
  16.9 0.0 copy-done
  16.9 0.0 copy-done.1
  16.9 2.5 %collective-permute-start = (bf16[2,64,256]{2,1,0:T(8,128)(2,1)S(1)}, bf16[2,64,256]{2,1,0:T(8,128)(2,1)S(1)}, u32[]{:S(2)}, u32[]{:S(2)}) collective-permute-start(bf16[2,64,256]{2,1,0:T(8,128)(2,1)S(1)} %pad_maximum_fusion.4), channel_id=1, source_target_pairs={{8,0},{16,8},{24,16},{32,24},{40,32},{48,40},{56,48},{64,56},{72,6... | collective-permute-start | bytes 196616 | tf_op jit(solution)/shard_map/ppermute | solution.py:186
  19.5 0.1 copy.13
  19.6 0.1 reshape.77
  19.8 2.0 shard_map.94.blank
  21.8 9.4 %collective-permute-done = bf16[2,64,256]{2,1,0:T(8,128)(2,1)S(1)} collective-permute-done((bf16[2,64,256]{2,1,0:T(8,128)(2,1)S(1)}, bf16[2,64,256]{2,1,0:T(8,128)(2,1)S(1)}, u32[]{:S(2)}, u32[]{:S(2)}) %collective-permute-start) | collective-permute-done | bytes 65568 | tf_op jit(solution)/shard_map/ppermute | solution.py:186
  31.3 81.0 %all-to-all-done.slots = bf16[64,128,256]{2,1,0:T(8,128)(2,1)} async-done(((bf16[64,128,256]{2,1,0:T(8,128)(2,1)}), bf16[64,128,256]{2,1,0:T(8,128)(2,1)}, u32[]{:S(2)}, u32[]{:S(2)}) %all-to-all-start) | async-done | bytes 4194336 | tf_op jit(solution)/shard_map/all_to_all | solution.py:192
  112.3 4.0 %shard_map.95 = (bf16[64,128,256]{2,1,0:T(8,128)(2,1)}, bf16[6,256,128]{2,1,0:T(8,128)(2,1)S(1)}, bf16[6,256,128]{2,1,0:T(8,128)(2,1)S(1)}) custom-call(s32[24]{0:T(128)S(1)} %fusion.1.source, bf16[384,256]{1,0:T(8,128)(2,1)S(1)} %pad_maximum_fusion.queries, bf16[384,256]{1,0:T(8,128)(2,1)S(1)} %pad_maximum_fusion.1.grads, ...), custom_call_target="tpu_custom_call", output_to_operand_aliasing={{0}: (4, {})} | custom-call | flops 402653184 | bytes 4194304 | tf_op jit(solution)/shard_map/pallas_call | solution.py:238
  116.3 6.4 %all-to-all-start.1 = ((bf16[64,128,256]{2,1,0:T(8,128)(2,1)}), bf16[64,128,256]{2,1,0:T(8,128)(2,1)}, u32[]{:S(2)}, u32[]{:S(2)}) async-start(bf16[64,128,256]{2,1,0:T(8,128)(2,1)} %get-tuple-element.15), calls=%async_computation.1 | async-start | bytes 8388608 | tf_op jit(solution)/shard_map/all_to_all | solution.py:192
  122.7 0.0 copy-start.3
  122.8 2.9 %shard_map.96 = (bf16[384,256]{1,0:T(8,128)(2,1)S(1)}, bf16[384,256]{1,0:T(8,128)(2,1)S(1)}) custom-call(s32[24]{0:T(128)S(1)} %fusion.1.source, bf16[6,256,128]{2,1,0:T(8,128)(2,1)S(1)} %get-tuple-element.11.probs, bf16[6,256,128]{2,1,0:T(8,128)(2,1)S(1)} %get-tuple-element.12.scores_grad, bf16[64,128,256]{2,1,0:T(8,128)(2,1)} %all-to-all-done.slots), custom_call_target="tpu_custom_call" | custom-call | flops 201326592 | bytes 4194304 | tf_op jit(solution)/shard_map/pallas_call | solution.py:245
  125.7 3.5 %collective-permute-start.1 = (bf16[2,64,256]{2,1,0:T(8,128)(2,1)S(1)}, bf16[2,64,256]{2,1,0:T(8,128)(2,1)S(1)}, u32[]{:S(2)}, u32[]{:S(2)}) collective-permute-start(bf16[2,64,256]{2,1,0:T(8,128)(2,1)S(1)} %pad_maximum_fusion.5), channel_id=1, source_target_pairs={{0,8},{8,16},{16,24},{24,32},{32,40},{40,48},{48,56},{56,64},{64,7... | collective-permute-start | bytes 196616 | tf_op jit(solution)/shard_map/ppermute | solution.py:186
  129.3 0.6 select_reduce_fusion.which
  130.0 4.3 %collective-permute-done.1 = bf16[2,64,256]{2,1,0:T(8,128)(2,1)S(1)} collective-permute-done((bf16[2,64,256]{2,1,0:T(8,128)(2,1)S(1)}, bf16[2,64,256]{2,1,0:T(8,128)(2,1)S(1)}, u32[]{:S(2)}, u32[]{:S(2)}) %collective-permute-start.1) | collective-permute-done | bytes 65568 | tf_op jit(solution)/shard_map/ppermute | solution.py:186
  134.3 0.7 pad_maximum_fusion.3
  135.0 0.7 pad_maximum_fusion.2
  135.7 82.1 %all-to-all-done.1.slots = bf16[64,128,256]{2,1,0:T(8,128)(2,1)} async-done(((bf16[64,128,256]{2,1,0:T(8,128)(2,1)}), bf16[64,128,256]{2,1,0:T(8,128)(2,1)}, u32[]{:S(2)}, u32[]{:S(2)}) %all-to-all-start.1) | async-done | bytes 4194336 | tf_op jit(solution)/shard_map/all_to_all | solution.py:192
  217.9 2.9 %shard_map.97 = (bf16[24,64,256]{2,1,0:T(8,128)(2,1)}, bf16[24,64,256]{2,1,0:T(8,128)(2,1)}) custom-call(s32[24]{0:T(128)} %select_reduce_fusion.which, bf16[64,128,256]{2,1,0:T(8,128)(2,1)} %all-to-all-done.1.slots), custom_call_target="tpu_custom_call" | custom-call | bytes 4194304 | tf_op jit(solution)/shard_map/pallas_call | solution.py:254
  (17 shorter events, 0.2 us)
Async XLA Ops:
  4.8 12.0 %copy-start = (bf16[384,256]{1,0:T(8,128)(2,1)S(1)}, bf16[384,256]{1,0:T(8,128)(2,1)}, u32[]{:S(2)}) copy-start(bf16[384,256]{1,0:T(8,128)(2,1)} %param.6) | copy-start | bytes 589828
  4.8 12.0 %copy-start.1 = (bf16[384,256]{1,0:T(8,128)(2,1)S(1)}, bf16[384,256]{1,0:T(8,128)(2,1)}, u32[]{:S(2)}) copy-start(bf16[384,256]{1,0:T(8,128)(2,1)} %param.9) | copy-start | bytes 589828
  4.9 14.6 %copy-start.2 = (s32[6,4]{0,1:T(4,128)S(1)}, s32[6,4]{0,1:T(4,128)}, u32[]{:S(2)}) copy-start(s32[6,4]{0,1:T(4,128)} %param.10) | copy-start | bytes 292
  4.9 107.5 %all-to-all-start = ((bf16[64,128,256]{2,1,0:T(8,128)(2,1)}), bf16[64,128,256]{2,1,0:T(8,128)(2,1)}, u32[]{:S(2)}, u32[]{:S(2)}) async-start(bf16[64,128,256]{2,1,0:T(8,128)(2,1)} %shard_map.93), calls=%async_computation | async-start | bytes 8388608 | tf_op jit(solution)/shard_map/all_to_all | solution.py:192
  16.9 14.3 %collective-permute-start = (bf16[2,64,256]{2,1,0:T(8,128)(2,1)S(1)}, bf16[2,64,256]{2,1,0:T(8,128)(2,1)S(1)}, u32[]{:S(2)}, u32[]{:S(2)}) collective-permute-start(bf16[2,64,256]{2,1,0:T(8,128)(2,1)S(1)} %pad_maximum_fusion.4), channel_id=1, source_target_pairs={{8,0},{16,8},{24,16},{32,24},{40,32},{48,40},{56,48},{64,56},{72,6... | collective-permute-start | bytes 196616 | tf_op jit(solution)/shard_map/ppermute | solution.py:186
  116.3 101.6 %all-to-all-start.1 = ((bf16[64,128,256]{2,1,0:T(8,128)(2,1)}), bf16[64,128,256]{2,1,0:T(8,128)(2,1)}, u32[]{:S(2)}, u32[]{:S(2)}) async-start(bf16[64,128,256]{2,1,0:T(8,128)(2,1)} %get-tuple-element.15), calls=%async_computation.1 | async-start | bytes 8388608 | tf_op jit(solution)/shard_map/all_to_all | solution.py:192
  122.7 6.6 %copy-start.3 = (s32[1,64,1]{1,2,0:T(1,128)S(1)}, s32[1,64,1]{1,2,0:T(1,128)}, u32[]{:S(2)}) copy-start(s32[1,64,1]{1,2,0:T(1,128)} %param.11) | copy-start | bytes 772
  125.7 8.5 %collective-permute-start.1 = (bf16[2,64,256]{2,1,0:T(8,128)(2,1)S(1)}, bf16[2,64,256]{2,1,0:T(8,128)(2,1)S(1)}, u32[]{:S(2)}, u32[]{:S(2)}) collective-permute-start(bf16[2,64,256]{2,1,0:T(8,128)(2,1)S(1)} %pad_maximum_fusion.5), channel_id=1, source_target_pairs={{0,8},{8,16},{16,24},{24,32},{32,40},{40,48},{48,56},{56,64},{64,7... | collective-permute-start | bytes 196616 | tf_op jit(solution)/shard_map/ppermute | solution.py:186

commit v7 on v6

--- a/solution.py
+++ b/solution.py
@@ -254,7 +254,7 @@
     key_grad, value_grad = call(
         unpack_kernel, [SM, HB], (HB, HB), (unit_out, unit_out),
         scratch=[staged, pltpu.VMEM((PAIR, cols), low), pltpu.SemaphoreType.DMA((4,)), sem, sem],
-        moved=slot_bytes, vmem=58,
+        moved=slot_bytes, vmem=8,
     )(which, returned)
     flat = (units * GROUP, cols)
     return (attended, query_grad, key_grad.reshape(flat), value_grad.reshape(flat))

time: 222 us -> 221 us (level)
  no operation moved by 1% of the time
where the time goes in v7:
time: 221 us
  waiting for transfers between devices  177 us (80%)
  starting transfers between devices  24.5 us (11%)
  Pallas kernels  15.9 us (7%)
    all_to_all x2, waiting for transfers between devices, exchange(): lax.all_to_all(slots, 'seq', split_axis=0, concat_axis=0, tiled=True, axi...  163 us
    all_to_all x2, starting transfers between devices, exchange(): lax.all_to_all(slots, 'seq', split_axis=0, concat_axis=0, tiled=True, axi...  18.4 us
    ppermute x2, waiting for transfers between devices, shift(): lax.ppermute(value, axis, [(at, at + steps) for at in range(first, last)])  14.2 us
    ppermute x2, starting transfers between devices, shift(): lax.ppermute(value, axis, [(at, at + steps) for at in range(first, last)])  6.09 us
  transfers between devices with their start and end apart: 4, of which 4 were waited for; matrix products, arithmetic and copies ran while one was open for 1% of the time, Pallas kernels for 2%

profile of v7, /device:TPU:1, one launch (start us, length us, event | category | flops | bytes accessed | tf_op | source)
XLA Modules:
  0.0 220.6 jit_solution(582469793119452432)
XLA Ops:
  0.6 4.2 %shard_map.93 = bf16[64,128,256]{2,1,0:T(8,128)(2,1)} custom-call(s32[64]{0:T(128)} %bitcast.23, bf16[24,64,256]{2,1,0:T(8,128)(2,1)} %bitcast.21, bf16[24,64,256]{2,1,0:T(8,128)(2,1)} %bitcast.22), custom_call_target="tpu_custom_call" | custom-call | bytes 8388608 | tf_op jit(solution)/shard_map/pallas_call | solution.py:217
  4.8 0.0 copy-start
  4.8 0.0 copy-start.1
  4.8 0.0 copy-start.2
  4.9 12.0 %all-to-all-start = ((bf16[64,128,256]{2,1,0:T(8,128)(2,1)}), bf16[64,128,256]{2,1,0:T(8,128)(2,1)}, u32[]{:S(2)}, u32[]{:S(2)}) async-start(bf16[64,128,256]{2,1,0:T(8,128)(2,1)} %shard_map.93), calls=%async_computation | async-start | bytes 8388608 | tf_op jit(solution)/shard_map/all_to_all | solution.py:192
  16.9 0.0 copy-done
  16.9 0.0 copy-done.1
  16.9 2.5 %collective-permute-start = (bf16[2,64,256]{2,1,0:T(8,128)(2,1)S(1)}, bf16[2,64,256]{2,1,0:T(8,128)(2,1)S(1)}, u32[]{:S(2)}, u32[]{:S(2)}) collective-permute-start(bf16[2,64,256]{2,1,0:T(8,128)(2,1)S(1)} %pad_maximum_fusion.4), channel_id=1, source_target_pairs={{8,0},{16,8},{24,16},{32,24},{40,32},{48,40},{56,48},{64,56},{72,6... | collective-permute-start | bytes 196616 | tf_op jit(solution)/shard_map/ppermute | solution.py:186
  19.5 0.1 copy.13
  19.6 0.1 reshape.77
  19.8 2.0 shard_map.94.blank
  21.8 9.4 %collective-permute-done = bf16[2,64,256]{2,1,0:T(8,128)(2,1)S(1)} collective-permute-done((bf16[2,64,256]{2,1,0:T(8,128)(2,1)S(1)}, bf16[2,64,256]{2,1,0:T(8,128)(2,1)S(1)}, u32[]{:S(2)}, u32[]{:S(2)}) %collective-permute-start) | collective-permute-done | bytes 65568 | tf_op jit(solution)/shard_map/ppermute | solution.py:186
  31.3 81.0 %all-to-all-done.slots = bf16[64,128,256]{2,1,0:T(8,128)(2,1)} async-done(((bf16[64,128,256]{2,1,0:T(8,128)(2,1)}), bf16[64,128,256]{2,1,0:T(8,128)(2,1)}, u32[]{:S(2)}, u32[]{:S(2)}) %all-to-all-start) | async-done | bytes 4194336 | tf_op jit(solution)/shard_map/all_to_all | solution.py:192
  112.3 4.0 %shard_map.95 = (bf16[64,128,256]{2,1,0:T(8,128)(2,1)}, bf16[6,256,128]{2,1,0:T(8,128)(2,1)S(1)}, bf16[6,256,128]{2,1,0:T(8,128)(2,1)S(1)}) custom-call(s32[24]{0:T(128)S(1)} %fusion.1.source, bf16[384,256]{1,0:T(8,128)(2,1)S(1)} %pad_maximum_fusion.queries, bf16[384,256]{1,0:T(8,128)(2,1)S(1)} %pad_maximum_fusion.1.grads, ...), custom_call_target="tpu_custom_call", output_to_operand_aliasing={{0}: (4, {})} | custom-call | flops 402653184 | bytes 4194304 | tf_op jit(solution)/shard_map/pallas_call | solution.py:238
  116.3 6.4 %all-to-all-start.1 = ((bf16[64,128,256]{2,1,0:T(8,128)(2,1)}), bf16[64,128,256]{2,1,0:T(8,128)(2,1)}, u32[]{:S(2)}, u32[]{:S(2)}) async-start(bf16[64,128,256]{2,1,0:T(8,128)(2,1)} %get-tuple-element.15), calls=%async_computation.1 | async-start | bytes 8388608 | tf_op jit(solution)/shard_map/all_to_all | solution.py:192
  122.7 0.0 copy-start.3
  122.7 2.9 %shard_map.96 = (bf16[384,256]{1,0:T(8,128)(2,1)S(1)}, bf16[384,256]{1,0:T(8,128)(2,1)S(1)}) custom-call(s32[24]{0:T(128)S(1)} %fusion.1.source, bf16[6,256,128]{2,1,0:T(8,128)(2,1)S(1)} %get-tuple-element.11.probs, bf16[6,256,128]{2,1,0:T(8,128)(2,1)S(1)} %get-tuple-element.12.scores_grad, bf16[64,128,256]{2,1,0:T(8,128)(2,1)} %all-to-all-done.slots), custom_call_target="tpu_custom_call" | custom-call | flops 201326592 | bytes 4194304 | tf_op jit(solution)/shard_map/pallas_call | solution.py:245
  125.7 3.5 %collective-permute-start.1 = (bf16[2,64,256]{2,1,0:T(8,128)(2,1)S(1)}, bf16[2,64,256]{2,1,0:T(8,128)(2,1)S(1)}, u32[]{:S(2)}, u32[]{:S(2)}) collective-permute-start(bf16[2,64,256]{2,1,0:T(8,128)(2,1)S(1)} %pad_maximum_fusion.5), channel_id=1, source_target_pairs={{0,8},{8,16},{16,24},{24,32},{32,40},{40,48},{48,56},{56,64},{64,7... | collective-permute-start | bytes 196616 | tf_op jit(solution)/shard_map/ppermute | solution.py:186
  129.3 0.1 select_reduce_fusion.which
  129.4 4.8 %collective-permute-done.1 = bf16[2,64,256]{2,1,0:T(8,128)(2,1)S(1)} collective-permute-done((bf16[2,64,256]{2,1,0:T(8,128)(2,1)S(1)}, bf16[2,64,256]{2,1,0:T(8,128)(2,1)S(1)}, u32[]{:S(2)}, u32[]{:S(2)}) %collective-permute-start.1) | collective-permute-done | bytes 65568 | tf_op jit(solution)/shard_map/ppermute | solution.py:186
  134.3 0.7 pad_maximum_fusion.3
  135.0 0.7 pad_maximum_fusion.2
  135.7 82.1 %all-to-all-done.1.slots = bf16[64,128,256]{2,1,0:T(8,128)(2,1)} async-done(((bf16[64,128,256]{2,1,0:T(8,128)(2,1)}), bf16[64,128,256]{2,1,0:T(8,128)(2,1)}, u32[]{:S(2)}, u32[]{:S(2)}) %all-to-all-start.1) | async-done | bytes 4194336 | tf_op jit(solution)/shard_map/all_to_all | solution.py:192
  217.9 2.8 %shard_map.97 = (bf16[24,64,256]{2,1,0:T(8,128)(2,1)}, bf16[24,64,256]{2,1,0:T(8,128)(2,1)}) custom-call(s32[24]{0:T(128)S(1)} %select_reduce_fusion.which, bf16[64,128,256]{2,1,0:T(8,128)(2,1)} %all-to-all-done.1.slots), custom_call_target="tpu_custom_call" | custom-call | bytes 4194304 | tf_op jit(solution)/shard_map/pallas_call | solution.py:254
  (17 shorter events, 0.2 us)
Async XLA Ops:
  4.8 12.0 %copy-start = (bf16[384,256]{1,0:T(8,128)(2,1)S(1)}, bf16[384,256]{1,0:T(8,128)(2,1)}, u32[]{:S(2)}) copy-start(bf16[384,256]{1,0:T(8,128)(2,1)} %param.6) | copy-start | bytes 589828
  4.8 12.0 %copy-start.1 = (bf16[384,256]{1,0:T(8,128)(2,1)S(1)}, bf16[384,256]{1,0:T(8,128)(2,1)}, u32[]{:S(2)}) copy-start(bf16[384,256]{1,0:T(8,128)(2,1)} %param.9) | copy-start | bytes 589828
  4.8 14.6 %copy-start.2 = (s32[6,4]{0,1:T(4,128)S(1)}, s32[6,4]{0,1:T(4,128)}, u32[]{:S(2)}) copy-start(s32[6,4]{0,1:T(4,128)} %param.10) | copy-start | bytes 292
  4.9 107.5 %all-to-all-start = ((bf16[64,128,256]{2,1,0:T(8,128)(2,1)}), bf16[64,128,256]{2,1,0:T(8,128)(2,1)}, u32[]{:S(2)}, u32[]{:S(2)}) async-start(bf16[64,128,256]{2,1,0:T(8,128)(2,1)} %shard_map.93), calls=%async_computation | async-start | bytes 8388608 | tf_op jit(solution)/shard_map/all_to_all | solution.py:192
  16.9 14.3 %collective-permute-start = (bf16[2,64,256]{2,1,0:T(8,128)(2,1)S(1)}, bf16[2,64,256]{2,1,0:T(8,128)(2,1)S(1)}, u32[]{:S(2)}, u32[]{:S(2)}) collective-permute-start(bf16[2,64,256]{2,1,0:T(8,128)(2,1)S(1)} %pad_maximum_fusion.4), channel_id=1, source_target_pairs={{8,0},{16,8},{24,16},{32,24},{40,32},{48,40},{56,48},{64,56},{72,6... | collective-permute-start | bytes 196616 | tf_op jit(solution)/shard_map/ppermute | solution.py:186
  116.3 101.6 %all-to-all-start.1 = ((bf16[64,128,256]{2,1,0:T(8,128)(2,1)}), bf16[64,128,256]{2,1,0:T(8,128)(2,1)}, u32[]{:S(2)}, u32[]{:S(2)}) async-start(bf16[64,128,256]{2,1,0:T(8,128)(2,1)} %get-tuple-element.15), calls=%async_computation.1 | async-start | bytes 8388608 | tf_op jit(solution)/shard_map/all_to_all | solution.py:192
  122.7 6.6 %copy-start.3 = (s32[1,64,1]{1,2,0:T(1,128)S(1)}, s32[1,64,1]{1,2,0:T(1,128)}, u32[]{:S(2)}) copy-start(s32[1,64,1]{1,2,0:T(1,128)} %param.11) | copy-start | bytes 772
  125.7 8.5 %collective-permute-start.1 = (bf16[2,64,256]{2,1,0:T(8,128)(2,1)S(1)}, bf16[2,64,256]{2,1,0:T(8,128)(2,1)S(1)}, u32[]{:S(2)}, u32[]{:S(2)}) collective-permute-start(bf16[2,64,256]{2,1,0:T(8,128)(2,1)S(1)} %pad_maximum_fusion.5), channel_id=1, source_target_pairs={{0,8},{8,16},{16,24},{24,32},{32,40},{40,48},{48,56},{56,64},{64,7... | collective-permute-start | bytes 196616 | tf_op jit(solution)/shard_map/ppermute | solution.py:186
